TPU v7x, 32 devices: a whole 2x2x4 slice. The times are simulated.
32 devices in a mesh: groups: 2 (over x), space: 16 (over z, y, core).
Axes of the slice: x: 2, y: 2, z: 4, core: 2. Of those that a mesh axis runs over, the one named last changes fastest.
Arguments:
- signal: float32 [65536, 128], P(('groups', 'space')), parts along dimension 0, may hold values from -12 to 12
- space_tiles: float32 [512, 64, 384], P('space'), may hold values from -0.3125 to 0.3125
- tree_precision: float32 [256, 128], P('groups'), parts along dimension 0, may hold values from -0.5 to 0.5
- send_tiles: int32 [16, 4, 8], P('space'), may hold values from 0 to 31, as said below
- column_tiles: int32 [512, 6], P('space'), may hold values from 0 to 63, as said below
Outputs:
- product: float32 [65536, 128], P(('groups', 'space')), parts along dimension 0
- quad_form: float32 [2], P('groups'), parts along dimension 0
There are 2 independent parts, one for each index of `groups`. A program takes and returns all parts, laid end to end along the dimension named above; an argument that names none is the same for every part. Nothing has to cross between parts.
Inputs may be any that keep to these rules, and one draw needn't show every extreme that they name: `send_tiles`: within one list the tile numbers are distinct; a partition lists tiles only towards neighbours that exist on the grid, from 1 to 8 of them, and some partition lists 8 tiles east and another south; slots past a list's length hold other tiles. `column_tiles`: entry 0 of every tile row is the row's own tile; entries below 32 are the partition's own tiles; an entry 32 + d * 8 + j names slot j of the list received from direction d, and only slots within that list's length.
All inputs are finite; a program needn't handle non-finite values.
Results may differ from a plain program's by a relative error of at most 0.00022.
Values sent between devices are 32-bit elements; how exact they have to be, the bound alone decides.
A program may use at most 64 MiB of HBM per device.

v0:
```python
import jax
import jax.numpy as jnp
from jax import lax
from jax.sharding import PartitionSpec as P


def from_behind(block, axis, distance):
    devices = range(lax.axis_size(axis))
    route = [(i - distance, i) for i in devices if i - distance in devices]
    return lax.ppermute(block, axis, route)


def receive_lists(tiled, lists, wide):
    offsets = [1, -1, wide, -wide]
    pieces = []
    for direction in range(4):
        outgoing = tiled[lists[direction]]
        pieces.append(from_behind(outgoing, "space", offsets[direction]))
    return jnp.concatenate(pieces, axis=0)


def on_device(signal, space_tiles, tree_precision, send_tiles, column_tiles):
    count = lax.axis_size("space")
    wide = count // 8
    tile_rows = space_tiles.shape[0]
    tile_nodes = space_tiles.shape[1]
    stored = space_tiles.shape[2] // tile_nodes
    species = signal.shape[1]
    tiled = signal.reshape(tile_rows, tile_nodes, species)
    lists = send_tiles[0]
    received = receive_lists(tiled, lists, wide)
    extended = jnp.concatenate([tiled, received], axis=0)
    gathered = extended[column_tiles].reshape(tile_rows, stored * tile_nodes, species)
    spatial = jnp.einsum("rac,rcs->ras", space_tiles, gathered, precision=lax.Precision.HIGHEST)
    spatial = spatial.reshape(tile_rows * tile_nodes, species)
    product = jnp.dot(
        spatial,
        tree_precision.T,
        precision=lax.Precision.HIGHEST,
        preferred_element_type=jnp.float32,
    )
    total = lax.psum(jnp.sum(signal * product), "space")
    scaling = jnp.sqrt(jnp.float32(count * tile_rows * tile_nodes * species))
    return (product, (total / scaling).reshape(1))


def solution(mesh):
    placed = (
        P(("groups", "space"), None),
        P("space", None, None),
        P("groups", None),
        P("space", None, None),
        P("space", None),
    )
    return jax.shard_map(
        on_device,
        mesh=mesh,
        in_specs=placed,
        out_specs=(P(("groups", "space"), None), P("groups")),
        check_vma=False,
    )
```

profile of v0, /device:TPU:0, one launch (start us, length us, event | category | flops | bytes accessed | tf_op | source)
XLA Modules:
  0.0 82.9 jit_solution(9771057362921722270)
XLA Ops:
  0.6 0.0 copy-start
  0.6 0.0 copy-start.3
  0.7 0.9 %fusion.3 = (s32[8]{0:T(128)S(1)}, s32[8]{0:T(128)S(1)}, s32[8]{0:T(128)S(1)}, s32[8]{0:T(128)S(1)}) fusion(s32[1,4,8]{2,1,0:T(4,128)} %param.8), kind=kLoop, calls=%fused_computation.24 | loop fusion | flops 96 | bytes 256 | tf_op jit(solution)/shard_map/select_n | solution.py:17
  1.6 1.9 %gather_fusion.3 = f32[8,64,128]{2,1,0:T(8,128)S(1)} fusion(f32[32,64,128]{2,1,0:T(8,128)} %bitcast.27, s32[1024]{0:T(1024)S(1)} %pad_clamp_fusion.1), kind=kCustom, calls=%fused_computation.3 | custom fusion | bytes 524320 | tf_op jit(solution)/shard_map/gather | solution.py:17
  3.5 1.3 %collective-permute-start.3 = (f32[8,64,128]{2,1,0:T(8,128)S(1)}, f32[8,64,128]{2,1,0:T(8,128)}, u32[]{:S(2)}, u32[]{:S(2)}) collective-permute-start(f32[8,64,128]{2,1,0:T(8,128)S(1)} %gather_fusion.3), channel_id=1, source_target_pairs={{2,0},{3,1},{4,2},{5,3},{6,4},{7,5},{8,6},{9,7},{10,8},{11,9},{12,... | collective-permute-start | bytes 786440 | tf_op jit(solution)/shard_map/ppermute | solution.py:10
  4.8 2.5 %gather_fusion.1 = f32[8,64,128]{2,1,0:T(8,128)} fusion(f32[32,64,128]{2,1,0:T(8,128)} %bitcast.28, s32[1024]{0:T(1024)S(1)} %pad_clamp_fusion.3), kind=kCustom, calls=%fused_computation.1 | custom fusion | bytes 524320 | tf_op jit(solution)/shard_map/gather | solution.py:17
  7.3 1.3 %collective-permute-start.1 = (f32[8,64,128]{2,1,0:T(8,128)}, f32[8,64,128]{2,1,0:T(8,128)}, u32[]{:S(2)}, u32[]{:S(2)}) collective-permute-start(f32[8,64,128]{2,1,0:T(8,128)} %gather_fusion.1), channel_id=1, source_target_pairs={{1,0},{2,1},{3,2},{4,3},{5,4},{6,5},{7,6},{8,7},{9,8},{10,9},{11,1... | collective-permute-start | bytes 786440 | tf_op jit(solution)/shard_map/ppermute | solution.py:10
  8.6 2.5 %gather_fusion = f32[8,64,128]{2,1,0:T(8,128)} fusion(f32[32,64,128]{2,1,0:T(8,128)} %bitcast.29, s32[1024]{0:T(1024)S(1)} %pad_clamp_fusion.4), kind=kCustom, calls=%fused_computation | custom fusion | bytes 524320 | tf_op jit(solution)/shard_map/gather | solution.py:17
  11.0 3.7 %collective-permute-start = (f32[8,64,128]{2,1,0:T(8,128)}, f32[8,64,128]{2,1,0:T(8,128)}, u32[]{:S(2)}, u32[]{:S(2)}) collective-permute-start(f32[8,64,128]{2,1,0:T(8,128)} %gather_fusion), channel_id=1, source_target_pairs={{0,1},{1,2},{2,3},{3,4},{4,5},{5,6},{6,7},{7,8},{8,9},{9,10},{10,1... | collective-permute-start | bytes 786440 | tf_op jit(solution)/shard_map/ppermute | solution.py:10
  14.8 2.5 %gather_fusion.2 = f32[8,64,128]{2,1,0:T(8,128)} fusion(f32[32,64,128]{2,1,0:T(8,128)} %bitcast.30, s32[1024]{0:T(1024)S(1)} %pad_clamp_fusion.2), kind=kCustom, calls=%fused_computation.2 | custom fusion | bytes 524320 | tf_op jit(solution)/shard_map/gather | solution.py:17
  17.3 5.5 %collective-permute-start.2 = (f32[8,64,128]{2,1,0:T(8,128)}, f32[8,64,128]{2,1,0:T(8,128)}, u32[]{:S(2)}, u32[]{:S(2)}) collective-permute-start(f32[8,64,128]{2,1,0:T(8,128)} %gather_fusion.2), channel_id=1, source_target_pairs={{0,2},{1,3},{2,4},{3,5},{4,6},{5,7},{6,8},{7,9},{8,10},{9,11},{10,... | collective-permute-start | bytes 786440 | tf_op jit(solution)/shard_map/ppermute | solution.py:10
  22.8 0.0 copy-done.3
  22.8 2.3 %constant_dynamic-update-slice_fusion.4 = f32[64,64,128]{2,1,0:T(8,128)} fusion(f32[32,64,128]{2,1,0:T(8,128)} %bitcast.31), kind=kLoop, calls=%fused_computation.11 | loop fusion | bytes 2097152
  25.1 0.1 copy.7
  25.2 0.1 reshape.174
  25.3 0.0 collective-permute-done
  25.3 1.7 %constant_dynamic-update-slice_fusion.3 = f32[64,64,128]{2,1,0:T(8,128)} fusion(f32[64,64,128]{2,1,0:T(8,128)} %constant_dynamic-update-slice_fusion.4, f32[8,64,128]{2,1,0:T(8,128)} %collective-permute-done), kind=kLoop, calls=%fused_computation.10 | loop fusion | bytes 524288
  27.0 0.0 collective-permute-done.1
  27.0 1.7 %constant_dynamic-update-slice_fusion.2 = f32[64,64,128]{2,1,0:T(8,128)} fusion(f32[64,64,128]{2,1,0:T(8,128)} %constant_dynamic-update-slice_fusion.3, f32[8,64,128]{2,1,0:T(8,128)} %collective-permute-done.1), kind=kLoop, calls=%fused_computation.9 | loop fusion | bytes 524288
  28.7 0.0 collective-permute-done.2
  28.7 1.7 %constant_dynamic-update-slice_fusion.1 = f32[64,64,128]{2,1,0:T(8,128)} fusion(f32[64,64,128]{2,1,0:T(8,128)} %constant_dynamic-update-slice_fusion.2, f32[8,64,128]{2,1,0:T(8,128)} %collective-permute-done.2), kind=kLoop, calls=%fused_computation.8 | loop fusion | bytes 524288
  30.4 0.0 collective-permute-done.3
  30.4 1.7 %constant_dynamic-update-slice_fusion = f32[64,64,128]{2,1,0:T(8,128)} fusion(f32[64,64,128]{2,1,0:T(8,128)} %constant_dynamic-update-slice_fusion.1, f32[8,64,128]{2,1,0:T(8,128)} %collective-permute-done.3), kind=kLoop, calls=%fused_computation.7 | loop fusion | bytes 524288 | tf_op jit(solution)/shard_map/concatenate | solution.py:32
  32.1 5.2 %gather_fusion.4 = f32[192,64,128]{2,1,0:T(8,128)} fusion(f32[64,64,128]{2,1,0:T(8,128)} %constant_dynamic-update-slice_fusion, s32[1024]{0:T(1024)S(1)} %pad_clamp_fusion), kind=kCustom, calls=%fused_computation.4 | custom fusion | bytes 12583680 | tf_op jit(solution)/shard_map/gather | solution.py:33
  37.3 0.0 copy-done
  37.3 0.0 copy-start.1
  37.3 0.0 copy-start.2
  37.3 6.8 %fusion.4 = f32[32,128,64]{1,2,0:T(8,128)S(1)} fusion(f32[32,384,128]{2,1,0:T(8,128)} %bitcast.26, f32[32,64,384]{2,1,0:T(8,128)S(1)} %copy-done), kind=kOutput, calls=%fused_computation.25 | convolution fusion | flops 1207959552 | bytes 10485760 | tf_op jit(solution)/shard_map/rac,rcs->ras/dot_general | solution.py:34
  44.1 0.0 copy-done.1
  44.1 0.0 copy-done.2
  44.2 2.6 %multiply_reduce_fusion = (f32[]{:T(128)}, f32[2048,128]{1,0:T(8,128)}) fusion(f32[2048,128]{1,0:T(8,128)S(1)} %copy-done.1, f32[2048,128]{1,0:T(8,128)S(1)} %bitcast.32, f32[128,128]{1,0:T(8,128)S(1)} %copy-done.2), kind=kOutput, calls=%fused_computation.5 | convolution fusion | flops 403177472 | bytes 3211268 | tf_op jit(solution)/shard_map/dot_general | solution.py:36
  46.8 34.3 %psum.7 = f32[]{:T(128)} all-reduce(f32[]{:T(128)} %get-tuple-element.6), channel_id=1, replica_groups=mesh['groups'=2,'space'=16] {'space'}, use_global_device_ids=true, to_apply=%region_1.0 | all-reduce | flops 1 | bytes 8 | tf_op jit(solution)/shard_map/psum | solution.py:42
  (6 shorter events, 0.0 us)
Async XLA Ops:
  0.6 36.7 %copy-start = (f32[32,64,384]{2,1,0:T(8,128)S(1)}, f32[32,64,384]{2,1,0:T(8,128)}, u32[]{:S(2)}) copy-start(f32[32,64,384]{2,1,0:T(8,128)} %param.6) | copy-start | bytes 9437188
  0.6 22.1 %copy-start.3 = (s32[32,6]{0,1:T(8,128)S(1)}, s32[32,6]{0,1:T(8,128)}, u32[]{:S(2)}) copy-start(s32[32,6]{0,1:T(8,128)} %param.9) | copy-start | bytes 2308
  3.5 26.9 %collective-permute-start.3 = (f32[8,64,128]{2,1,0:T(8,128)S(1)}, f32[8,64,128]{2,1,0:T(8,128)}, u32[]{:S(2)}, u32[]{:S(2)}) collective-permute-start(f32[8,64,128]{2,1,0:T(8,128)S(1)} %gather_fusion.3), channel_id=1, source_target_pairs={{2,0},{3,1},{4,2},{5,3},{6,4},{7,5},{8,6},{9,7},{10,8},{11,9},{12,... | collective-permute-start | bytes 786440 | tf_op jit(solution)/shard_map/ppermute | solution.py:10
  7.3 19.8 %collective-permute-start.1 = (f32[8,64,128]{2,1,0:T(8,128)}, f32[8,64,128]{2,1,0:T(8,128)}, u32[]{:S(2)}, u32[]{:S(2)}) collective-permute-start(f32[8,64,128]{2,1,0:T(8,128)} %gather_fusion.1), channel_id=1, source_target_pairs={{1,0},{2,1},{3,2},{4,3},{5,4},{6,5},{7,6},{8,7},{9,8},{10,9},{11,1... | collective-permute-start | bytes 786440 | tf_op jit(solution)/shard_map/ppermute | solution.py:10
  11.0 14.3 %collective-permute-start = (f32[8,64,128]{2,1,0:T(8,128)}, f32[8,64,128]{2,1,0:T(8,128)}, u32[]{:S(2)}, u32[]{:S(2)}) collective-permute-start(f32[8,64,128]{2,1,0:T(8,128)} %gather_fusion), channel_id=1, source_target_pairs={{0,1},{1,2},{2,3},{3,4},{4,5},{5,6},{6,7},{7,8},{8,9},{9,10},{10,1... | collective-permute-start | bytes 786440 | tf_op jit(solution)/shard_map/ppermute | solution.py:10
  17.3 11.4 %collective-permute-start.2 = (f32[8,64,128]{2,1,0:T(8,128)}, f32[8,64,128]{2,1,0:T(8,128)}, u32[]{:S(2)}, u32[]{:S(2)}) collective-permute-start(f32[8,64,128]{2,1,0:T(8,128)} %gather_fusion.2), channel_id=1, source_target_pairs={{0,2},{1,3},{2,4},{3,5},{4,6},{5,7},{6,8},{7,9},{8,10},{9,11},{10,... | collective-permute-start | bytes 786440 | tf_op jit(solution)/shard_map/ppermute | solution.py:10
  37.3 6.9 %copy-start.1 = (f32[2048,128]{1,0:T(8,128)S(1)}, f32[2048,128]{1,0:T(8,128)}, u32[]{:S(2)}) copy-start(f32[2048,128]{1,0:T(8,128)} %param.5) | copy-start | bytes 3145732
  37.3 6.9 %copy-start.2 = (f32[128,128]{1,0:T(8,128)S(1)}, f32[128,128]{1,0:T(8,128)}, u32[]{:S(2)}) copy-start(f32[128,128]{1,0:T(8,128)} %param.7) | copy-start | bytes 196612
where the time goes:
time: 83.4 us; the launch traced here: 82.9 us
  blocking collectives  34.3 us (41%)
  local copies, waits for them, and re-layouts  23.8 us (29%)
  starting transfers between devices  11.8 us (14%)
  matrix products  9.46 us (11%)
  between operations  2.52 us (3%)
  other arithmetic  0.92 us (1%)
    psum x1, blocking collectives, on_device(): total = lax.psum(jnp.sum(signal * product), 'space')  34.3 us
    ppermute x4, starting transfers between devices, from_behind(): return lax.ppermute(block, axis, route)  11.8 us
    gather x4, local copies, waits for them, and re-layouts, receive_lists(): outgoing = tiled[lists[direction]]  9.36 us
    unnamed x12, local copies, waits for them, and re-layouts  7.37 us
    dot_general x1, matrix products, on_device(): jnp.einsum('rac,rcs->ras', space_tiles, gathered, precision=lax.Precision...  6.84 us
    gather x1, local copies, waits for them, and re-layouts, on_device(): extended[column_tiles].reshape(tile_rows, stored * tile_nodes, species)  5.2 us
    dot_general x1, matrix products, on_device(): jnp.dot(spatial, tree_precision.T, precision=lax.Precision.HIGHEST, prefe...  2.62 us
    concatenate x1, local copies, waits for them, and re-layouts, on_device(): extended = jnp.concatenate([tiled, received], axis=0)  1.71 us
  transfers between devices with their start and end apart: 4, of which 0 were waited for; matrix products, arithmetic and copies ran while one was open for 18% of the time, Pallas kernels for 0%

commit v1 on v0

v1 whole, which is shorter than its diff:
```python
import functools
import math

import jax
import jax.numpy as jnp
from jax import lax
from jax.experimental import pallas as pl
from jax.experimental.pallas import tpu as pltpu
from jax.sharding import PartitionSpec as P

ROWS = 8
CHUNKS = 4
MESH = pl.DeviceIdType.MESH


def halves(value):
    high = value.astype(jnp.bfloat16)
    low = (value - high.astype(jnp.float32)).astype(jnp.bfloat16)
    return high, low


def kernel(
    count, scaling,
    signal_ref, tiles_ref, tree_ref, send_ref, column_ref,
    product_ref, quad_ref,
    x, tiles, a, xs, z, spatial, outgoing, received, out, shares,
    x_sem, tiles_sem, send_sem, recv_sem, share_send, share_recv, out_sem,
):
    tile_rows, nodes, species = x.shape
    stored = column_ref.shape[1]
    capacity = send_ref.shape[1]
    wide = count // ROWS
    me = lax.axis_index("space")
    column, row = lax.rem(me, wide), me // wide
    not_first, not_last = column > 0, column < wide - 1
    above, below = row > 0, row < ROWS - 1
    sends = (not_last, not_first, below, above)
    receives = (not_first, not_last, above, below)
    targets = (me + 1, me - 1, me + wide, me - wide)

    load_x = pltpu.make_async_copy(signal_ref, x, x_sem)
    load_x.start()
    part = tile_rows // CHUNKS
    loads = []
    for c in range(CHUNKS):
        piece = pl.ds(c * part, part)
        loads.append(pltpu.make_async_copy(tiles_ref.at[piece], tiles.at[piece], tiles_sem.at[c]))
        loads[-1].start()

    barrier = pltpu.get_barrier_semaphore()

    def greet(i, carry):
        pl.semaphore_signal(
            barrier, inc=1, device_id={"space": lax.rem(me + i, count)}, device_id_type=MESH
        )
        return carry

    lax.fori_loop(1, count, greet, 0)

    load_x.wait()

    def copy_for(d):
        return pltpu.make_async_remote_copy(
            src_ref=outgoing.at[d],
            dst_ref=received.at[d],
            send_sem=send_sem.at[d],
            recv_sem=recv_sem.at[d],
            device_id={"space": targets[d]},
            device_id_type=MESH,
        )

    for d in (2, 3, 0, 1):
        for j in range(capacity):
            outgoing[d, j] = x[send_ref[d, j]]
    pl.semaphore_wait(barrier, count - 1)
    for d in (2, 3, 0, 1):
        @pl.when(sends[d])
        def _():
            copy_for(d).start()

    tree = tree_ref[...]
    zero = jnp.zeros((species, species), jnp.bfloat16)

    def doubled(matrix):
        high, low = halves(matrix)
        return jnp.concatenate(
            [jnp.concatenate([high, low], 1), jnp.concatenate([high, zero], 1)], 0
        )

    def times(paired, weights):
        both = jnp.dot(paired, weights, preferred_element_type=jnp.float32)
        return both[:, :species] + both[:, species:]

    right, right_t = doubled(tree), doubled(tree.T)

    def prepare(t, carry):
        high, low = halves(x[t])
        paired = jnp.concatenate([high, low], 1)
        xs[t] = paired
        z[t] = times(paired, right)
        return carry

    lax.fori_loop(0, tile_rows, prepare, 0)
    for load in loads:
        load.wait()

    def cut(t, carry):
        high, low = halves(tiles[t])
        a[t] = jnp.concatenate([high, low], 0)
        return carry

    lax.fori_loop(0, tile_rows, cut, 0)

    for d in (0, 1, 2, 3):
        @pl.when(receives[d])
        def _():
            copy_for(d).wait_recv()
            for j in range(capacity):
                high, low = halves(received[d, j])
                xs[tile_rows + d * capacity + j] = jnp.concatenate([high, low], 1)

    def multiply(t, acc):
        block = jnp.concatenate([xs[column_ref[t, k]] for k in range(stored)], 0)
        both = jnp.dot(a[t], block, preferred_element_type=jnp.float32)
        small = both[:nodes, species:] + both[nodes:, :species] + both[nodes:, species:]
        result = both[:nodes, :species] + small
        spatial[t] = result
        return acc + jnp.sum((z[t] * result).reshape(nodes // 8, 8, species), axis=0)

    acc = lax.fori_loop(
        0, tile_rows, multiply, jnp.zeros((8, species), jnp.float32), unroll=4
    )

    shares[me] = acc

    def share_copy(i):
        return pltpu.make_async_remote_copy(
            src_ref=shares.at[me],
            dst_ref=shares.at[me],
            send_sem=share_send.at[i],
            recv_sem=share_recv.at[i],
            device_id={"space": lax.rem(me + i, count)},
            device_id_type=MESH,
        )

    def give(i, carry):
        share_copy(i).start()
        return carry

    lax.fori_loop(1, count, give, 0)

    stores = []
    for c in range(CHUNKS):
        piece = pl.ds(c * part, part)
        high, low = halves(spatial[piece].reshape(part * nodes, species))
        result = times(jnp.concatenate([high, low], 1), right_t)
        out[piece] = result.reshape(part, nodes, species)
        stores.append(pltpu.make_async_copy(out.at[piece], product_ref.at[piece], out_sem.at[c]))
        stores[-1].start()

    for d in range(4):
        @pl.when(sends[d])
        def _():
            copy_for(d).wait_send()

    def take(i, carry):
        share_copy(i).wait_recv()
        return carry

    lax.fori_loop(1, count, take, 0)

    def sent(i, carry):
        share_copy(i).wait_send()
        return carry

    lax.fori_loop(1, count, sent, 0)
    quad_ref[0] = jnp.sum(jnp.sum(shares[...], axis=0)) * scaling
    for store in stores:
        store.wait()


def on_device(signal, space_tiles, tree_precision, send_tiles, column_tiles):
    count = lax.axis_size("space")
    tile_rows, nodes, width = space_tiles.shape
    species = signal.shape[1]
    directions, capacity = send_tiles.shape[1:]
    scaling = 1.0 / math.sqrt(count * tile_rows * nodes * species)
    vmem, f32, bf16 = pltpu.VMEM, jnp.float32, jnp.bfloat16
    dma = pltpu.SemaphoreType.DMA
    everywhere = pl.BlockSpec(memory_space=pl.ANY)
    smem = pl.BlockSpec(memory_space=pltpu.SMEM)
    field = (tile_rows, nodes, species)
    lists = (directions, capacity, nodes, species)
    product, quad = pl.pallas_call(
        functools.partial(kernel, count, scaling),
        out_shape=(jax.ShapeDtypeStruct(field, f32), jax.ShapeDtypeStruct((1,), f32)),
        in_specs=[everywhere, everywhere, pl.BlockSpec(memory_space=vmem), smem, smem],
        out_specs=(everywhere, smem),
        scratch_shapes=[
            vmem(field, f32),
            vmem(space_tiles.shape, f32),
            vmem((tile_rows, 2 * nodes, width), bf16),
            vmem((tile_rows + directions * capacity, nodes, 2 * species), bf16),
            vmem(field, f32),
            vmem(field, f32),
            vmem(lists, f32),
            vmem(lists, f32),
            vmem(field, f32),
            vmem((count, 8, species), f32),
            dma,
            dma((CHUNKS,)),
            dma((directions,)),
            dma((directions,)),
            dma((count,)),
            dma((count,)),
            dma((CHUNKS,)),
        ],
        compiler_params=pltpu.CompilerParams(
            collective_id=0, has_side_effects=True, vmem_limit_bytes=40 * 2**20
        ),
        cost_estimate=pl.CostEstimate(
            flops=2 * tile_rows * nodes * species * (width + 2 * species),
            bytes_accessed=4 * (space_tiles.size + 2 * signal.size),
            transcendentals=0,
        ),
        name="kronecker_product",
    )(signal.reshape(field), space_tiles, tree_precision, send_tiles[0], column_tiles)
    return product.reshape(signal.shape), quad


def solution(mesh):
    placed = (
        P(("groups", "space"), None),
        P("space", None, None),
        P("groups", None),
        P("space", None, None),
        P("space", None),
    )
    return jax.shard_map(
        on_device,
        mesh=mesh,
        in_specs=placed,
        out_specs=(P(("groups", "space"), None), P("groups")),
        check_vma=False,
    )
```

time: 83.4 us -> 36.2 us (0.43)
  blocking collectives: 34.3 us -> 0 us
  Pallas kernels: 0 us -> 27.1 us
  local copies, waits for them, and re-layouts: 23.8 us -> 6.37 us
  starting transfers between devices: 11.8 us -> 0 us
  matrix products: 9.46 us -> 0 us
  other arithmetic: 0.92 us -> 0 us
    psum x1 -> x0, blocking collectives: 34.3 us -> none  [on_device(): total = lax.psum(jnp.sum(signal * product), 'space')]
    pallas_call x0 -> x1, Pallas kernels: none -> 27.1 us  [on_device(): pl.pallas_call(functools.partial(kernel, count, scaling), out_shape=(jax....]
    gather x5 -> x0, local copies, waits for them, and re-layouts: 14.6 us -> none  [the longest x4 9.36 us: receive_lists(): outgoing = tiled[lists[direction]]]
    ppermute x4 -> x0, starting transfers between devices: 11.8 us -> none  [from_behind(): return lax.ppermute(block, axis, route)]
    dot_general x2 -> x0, matrix products: 9.46 us -> none  [the longest x1 6.84 us: on_device(): jnp.einsum('rac,rcs->ras', space_tiles, gathered, precision=lax.Precision...]
    concatenate x1 -> x0, local copies, waits for them, and re-layouts: 1.71 us -> none  [on_device(): extended = jnp.concatenate([tiled, received], axis=0)]
    unnamed x12 -> x10, local copies, waits for them, and re-layouts: 7.37 us -> 6.37 us
    select_n x2 -> x0, other arithmetic: 0.89 us -> none  [the longest x1 0.89 us: receive_lists(): outgoing = tiled[lists[direction]]]
  transfers between devices with their start and end apart: 4 -> 0, of which waited for: 0 -> 0; matrix products, arithmetic and copies ran while one was open for 18% -> 0% of each run, Pallas kernels for 0% -> 0%
where the time goes in v1:
time: 36.2 us; the launch traced here: 35.9 us
  Pallas kernels  27.1 us (75%)
  local copies, waits for them, and re-layouts  6.37 us (18%)
  between operations  2.39 us (7%)
    pallas_call x1, Pallas kernels, on_device(): pl.pallas_call(functools.partial(kernel, count, scaling), out_shape=(jax....  27.1 us
    unnamed x10, local copies, waits for them, and re-layouts  6.37 us

profile of v1, /device:TPU:0, one launch (start us, length us, event | category | flops | bytes accessed | tf_op | source)
XLA Modules:
  0.0 35.9 jit_solution(9564205655386150736)
XLA Ops:
  0.6 0.8 %copy.7.column_ref = s32[32,6]{1,0:T(8,128)S(1)} copy(s32[32,6]{0,1:T(8,128)} %param.9) | data formatting | bytes 1536 | tf_op args[4]
  1.4 0.0 copy-start
  1.4 1.9 %copy-done = f32[32,64,384]{2,1,0:T(8,128)S(1)} copy-done((f32[32,64,384]{2,1,0:T(8,128)S(1)}, f32[32,64,384]{2,1,0:T(8,128)}, u32[]{:S(2)}) %copy-start) | copy-done | bytes 3145752
  3.3 0.0 copy-start.1
  3.3 1.2 %copy-done.1 = f32[2048,128]{1,0:T(8,128)S(1)} copy-done((f32[2048,128]{1,0:T(8,128)S(1)}, f32[2048,128]{1,0:T(8,128)}, u32[]{:S(2)}) %copy-start.1) | copy-done | bytes 1048600
  4.5 0.0 copy-start.2
  4.5 0.8 %copy-done.2 = f32[128,128]{1,0:T(8,128)S(1)} copy-done((f32[128,128]{1,0:T(8,128)S(1)}, f32[128,128]{1,0:T(8,128)}, u32[]{:S(2)}) %copy-start.2) | copy-done | bytes 65560
  5.4 0.0 copy-start.3
  5.4 0.7 %copy-done.3 = s32[1,4,8]{2,1,0:T(4,128)S(1)} copy-done((s32[1,4,8]{2,1,0:T(4,128)S(1)}, s32[1,4,8]{2,1,0:T(4,128)}, u32[]{:S(2)}) %copy-start.3) | copy-done | bytes 152
  6.0 27.1 %kronecker_product.1 = (f32[32,64,128]{2,1,0:T(8,128)S(1)}, f32[1]{0:T(128)}) custom-call(f32[32,64,128]{2,1,0:T(8,128)S(1)} %bitcast.4, f32[32,64,384]{2,1,0:T(8,128)S(1)} %copy-done, f32[128,128]{1,0:T(8,128)S(1)} %copy-done.2, s32[4,8]{1,0:T(4,128)S(1)} %bitcast.5, s32[32,6]{1,0:T(8,128)S(1)} %copy.7.column_ref), custom_call_target="tpu_custom_call" | custom-call | flops 335544320 | bytes 5242880 | tf_op jit(solution)/shard_map/kronecker_product/pallas_call | solution.py:194
  33.2 1.0 %copy.10 = f32[2048,128]{1,0:T(8,128)} copy(f32[2048,128]{1,0:T(8,128)S(1)} %bitcast.3) | data formatting | bytes 2097152
Async XLA Ops:
  1.4 1.9 %copy-start = (f32[32,64,384]{2,1,0:T(8,128)S(1)}, f32[32,64,384]{2,1,0:T(8,128)}, u32[]{:S(2)}) copy-start(f32[32,64,384]{2,1,0:T(8,128)} %tiles_ref.1) | copy-start | bytes 9437188
  3.3 1.2 %copy-start.1 = (f32[2048,128]{1,0:T(8,128)S(1)}, f32[2048,128]{1,0:T(8,128)}, u32[]{:S(2)}) copy-start(f32[2048,128]{1,0:T(8,128)} %param.5) | copy-start | bytes 3145732
  4.5 0.8 %copy-start.2 = (f32[128,128]{1,0:T(8,128)S(1)}, f32[128,128]{1,0:T(8,128)}, u32[]{:S(2)}) copy-start(f32[128,128]{1,0:T(8,128)} %tree_ref.1) | copy-start | bytes 196612
  5.4 0.7 %copy-start.3 = (s32[1,4,8]{2,1,0:T(4,128)S(1)}, s32[1,4,8]{2,1,0:T(4,128)}, u32[]{:S(2)}) copy-start(s32[1,4,8]{2,1,0:T(4,128)} %param.8) | copy-start | bytes 388

commit v2 on v1

--- a/solution.py
+++ b/solution.py
@@ -23,12 +23,20 @@
     count, scaling,
     signal_ref, tiles_ref, tree_ref, send_ref, column_ref,
     product_ref, quad_ref,
-    x, tiles, a, xs, z, spatial, outgoing, received, out, shares,
-    x_sem, tiles_sem, send_sem, recv_sem, share_send, share_recv, out_sem,
+    x, tiles, tree_in, send_in, column_in, a, xs, z, spatial, outgoing, received, shares,
+    x_sem, small_sem, tiles_sem, send_sem, recv_sem, share_send, share_recv,
 ):
     tile_rows, nodes, species = x.shape
-    stored = column_ref.shape[1]
+    stored = column_ref.shape[0]
     capacity = send_ref.shape[1]
+    load_send = pltpu.make_async_copy(send_ref, send_in, small_sem.at[0])
+    load_send.start()
+    load_x = pltpu.make_async_copy(signal_ref, x, x_sem)
+    load_x.start()
+    load_tree = pltpu.make_async_copy(tree_ref, tree_in, small_sem.at[1])
+    load_tree.start()
+    load_column = pltpu.make_async_copy(column_ref, column_in, small_sem.at[2])
+    load_column.start()
     wide = count // ROWS
     me = lax.axis_index("space")
     column, row = lax.rem(me, wide), me // wide
@@ -38,8 +46,6 @@
     receives = (not_first, not_last, above, below)
     targets = (me + 1, me - 1, me + wide, me - wide)
 
-    load_x = pltpu.make_async_copy(signal_ref, x, x_sem)
-    load_x.start()
     part = tile_rows // CHUNKS
     loads = []
     for c in range(CHUNKS):
@@ -57,6 +63,7 @@
 
     lax.fori_loop(1, count, greet, 0)
 
+    load_send.wait()
     load_x.wait()
 
     def copy_for(d):
@@ -71,14 +78,16 @@
 
     for d in (2, 3, 0, 1):
         for j in range(capacity):
-            outgoing[d, j] = x[send_ref[d, j]]
-    pl.semaphore_wait(barrier, count - 1)
-    for d in (2, 3, 0, 1):
+            outgoing[d, j] = x[send_in[d, j]]
+        if d == 2:
+            pl.semaphore_wait(barrier, count - 1)
+
         @pl.when(sends[d])
         def _():
             copy_for(d).start()
 
-    tree = tree_ref[...]
+    load_tree.wait()
+    tree = tree_in[...]
     zero = jnp.zeros((species, species), jnp.bfloat16)
 
     def doubled(matrix):
@@ -93,14 +102,16 @@
 
     right, right_t = doubled(tree), doubled(tree.T)
 
-    def prepare(t, carry):
-        high, low = halves(x[t])
-        paired = jnp.concatenate([high, low], 1)
-        xs[t] = paired
-        z[t] = times(paired, right)
-        return carry
-
-    lax.fori_loop(0, tile_rows, prepare, 0)
+    def prepare(c, carry):
+        piece = pl.ds(c * part, part)
+        high, low = halves(x[piece])
+        paired = jnp.concatenate([high, low], 2)
+        xs[piece] = paired
+        result = times(paired.reshape(part * nodes, 2 * species), right)
+        z[piece] = result.reshape(part, nodes, species)
+        return carry
+
+    lax.fori_loop(0, CHUNKS, prepare, 0)
     for load in loads:
         load.wait()
 
@@ -109,7 +120,8 @@
         a[t] = jnp.concatenate([high, low], 0)
         return carry
 
-    lax.fori_loop(0, tile_rows, cut, 0)
+    lax.fori_loop(0, tile_rows, cut, 0, unroll=4)
+    load_column.wait()
 
     for d in (0, 1, 2, 3):
         @pl.when(receives[d])
@@ -120,7 +132,7 @@
                 xs[tile_rows + d * capacity + j] = jnp.concatenate([high, low], 1)
 
     def multiply(t, acc):
-        block = jnp.concatenate([xs[column_ref[t, k]] for k in range(stored)], 0)
+        block = jnp.concatenate([xs[column_in[k, t]] for k in range(stored)], 0)
         both = jnp.dot(a[t], block, preferred_element_type=jnp.float32)
         small = both[:nodes, species:] + both[nodes:, :species] + both[nodes:, species:]
         result = both[:nodes, :species] + small
@@ -128,7 +140,7 @@
         return acc + jnp.sum((z[t] * result).reshape(nodes // 8, 8, species), axis=0)
 
     acc = lax.fori_loop(
-        0, tile_rows, multiply, jnp.zeros((8, species), jnp.float32), unroll=4
+        0, tile_rows, multiply, jnp.zeros((8, species), jnp.float32), unroll=8
     )
 
     shares[me] = acc
@@ -149,14 +161,11 @@
 
     lax.fori_loop(1, count, give, 0)
 
-    stores = []
     for c in range(CHUNKS):
         piece = pl.ds(c * part, part)
         high, low = halves(spatial[piece].reshape(part * nodes, species))
         result = times(jnp.concatenate([high, low], 1), right_t)
-        out[piece] = result.reshape(part, nodes, species)
-        stores.append(pltpu.make_async_copy(out.at[piece], product_ref.at[piece], out_sem.at[c]))
-        stores[-1].start()
+        product_ref[piece] = result.reshape(part, nodes, species)
 
     for d in range(4):
         @pl.when(sends[d])
@@ -175,8 +184,6 @@
 
     lax.fori_loop(1, count, sent, 0)
     quad_ref[0] = jnp.sum(jnp.sum(shares[...], axis=0)) * scaling
-    for store in stores:
-        store.wait()
 
 
 def on_device(signal, space_tiles, tree_precision, send_tiles, column_tiles):
@@ -187,33 +194,35 @@
     scaling = 1.0 / math.sqrt(count * tile_rows * nodes * species)
     vmem, f32, bf16 = pltpu.VMEM, jnp.float32, jnp.bfloat16
     dma = pltpu.SemaphoreType.DMA
-    everywhere = pl.BlockSpec(memory_space=pl.ANY)
+    hbm = pl.BlockSpec(memory_space=pltpu.HBM)
     smem = pl.BlockSpec(memory_space=pltpu.SMEM)
     field = (tile_rows, nodes, species)
     lists = (directions, capacity, nodes, species)
     product, quad = pl.pallas_call(
         functools.partial(kernel, count, scaling),
-        out_shape=(jax.ShapeDtypeStruct(field, f32), jax.ShapeDtypeStruct((1,), f32)),
-        in_specs=[everywhere, everywhere, pl.BlockSpec(memory_space=vmem), smem, smem],
-        out_specs=(everywhere, smem),
+        out_shape=(pltpu.VMEM(field, f32), jax.ShapeDtypeStruct((1,), f32)),
+        in_specs=[hbm] * 5,
+        out_specs=(pl.BlockSpec(memory_space=vmem), smem),
         scratch_shapes=[
             vmem(field, f32),
             vmem(space_tiles.shape, f32),
+            vmem(tree_precision.shape, f32),
+            pltpu.SMEM((directions, capacity), jnp.int32),
+            pltpu.SMEM(column_tiles.shape[::-1], jnp.int32),
             vmem((tile_rows, 2 * nodes, width), bf16),
             vmem((tile_rows + directions * capacity, nodes, 2 * species), bf16),
             vmem(field, f32),
             vmem(field, f32),
             vmem(lists, f32),
             vmem(lists, f32),
-            vmem(field, f32),
             vmem((count, 8, species), f32),
             dma,
+            dma((3,)),
             dma((CHUNKS,)),
             dma((directions,)),
             dma((directions,)),
             dma((count,)),
             dma((count,)),
-            dma((CHUNKS,)),
         ],
         compiler_params=pltpu.CompilerParams(
             collective_id=0, has_side_effects=True, vmem_limit_bytes=40 * 2**20
@@ -224,7 +233,10 @@
             transcendentals=0,
         ),
         name="kronecker_product",
-    )(signal.reshape(field), space_tiles, tree_precision, send_tiles[0], column_tiles)
+    )(*(
+        pltpu.with_memory_space_constraint(array, pltpu.HBM)
+        for array in (signal.reshape(field), space_tiles, tree_precision, send_tiles[0], column_tiles.T)
+    ))
     return product.reshape(signal.shape), quad
 
 

time: 36.2 us -> 28.9 us (0.80)
  local copies, waits for them, and re-layouts: 6.37 us -> 0.97 us
  Pallas kernels: 27.1 us -> 25.4 us
    unnamed x10 -> x1, local copies, waits for them, and re-layouts: 6.37 us -> 0.97 us
    pallas_call x1, Pallas kernels: 27.1 us -> 25.4 us  [on_device(): pl.pallas_call(functools.partial(kernel, count, scaling), out_shape=(pltp...]
where the time goes in v2:
time: 28.9 us; the launch traced here: 28.7 us
  Pallas kernels  25.4 us (88%)
  between operations  2.33 us (8%)
  local copies, waits for them, and re-layouts  0.97 us (3%)
    pallas_call x1, Pallas kernels, on_device(): pl.pallas_call(functools.partial(kernel, count, scaling), out_shape=(pltp...  25.4 us
    unnamed x1, local copies, waits for them, and re-layouts  0.97 us

profile of v2, /device:TPU:0, one launch (start us, length us, event | category | flops | bytes accessed | tf_op | source)
XLA Modules:
  0.0 28.7 jit_solution(16571660177106775450)
XLA Ops:
  0.6 25.4 %kronecker_product.1 = (f32[32,64,128]{2,1,0:T(8,128)S(1)}, f32[1]{0:T(128)}) custom-call(f32[32,64,128]{2,1,0:T(8,128)} %bitcast.5, f32[32,64,384]{2,1,0:T(8,128)} %tiles_ref.1, f32[128,128]{1,0:T(8,128)} %tree_ref.1, s32[4,8]{1,0:T(4,128)} %bitcast.7, s32[6,32]{1,0:T(8,128)} %bitcast.6), custom_call_target="tpu_custom_call" | custom-call | flops 335544320 | bytes 5242880 | tf_op jit(solution)/shard_map/kronecker_product/pallas_call | solution.py:201
  26.0 1.0 %copy.9 = f32[2048,128]{1,0:T(8,128)} copy(f32[2048,128]{1,0:T(8,128)S(1)} %bitcast.4) | data formatting | bytes 2097152

commit v3 on v2

--- a/solution.py
+++ b/solution.py
@@ -23,8 +23,9 @@
     count, scaling,
     signal_ref, tiles_ref, tree_ref, send_ref, column_ref,
     product_ref, quad_ref,
-    x, tiles, tree_in, send_in, column_in, a, xs, z, spatial, outgoing, received, shares,
-    x_sem, small_sem, tiles_sem, send_sem, recv_sem, share_send, share_recv,
+    x, tiles, tree_in, send_in, column_in, a, xs, extended, pull, outgoing, received,
+    inner_shares, outer_shares,
+    x_sem, small_sem, tiles_sem, send_sem, recv_sem, inner_send, inner_recv, outer_send, outer_recv,
 ):
     tile_rows, nodes, species = x.shape
     stored = column_ref.shape[0]
@@ -53,15 +54,21 @@
         loads.append(pltpu.make_async_copy(tiles_ref.at[piece], tiles.at[piece], tiles_sem.at[c]))
         loads[-1].start()
 
+    inner, outer = inner_shares.shape[0], outer_shares.shape[0]
+    spot, team = lax.rem(me, inner), me // inner
+    mates = [team * inner + lax.rem(spot + i, inner) for i in range(1, inner)]
+    peers = [spot + inner * lax.rem(team + i, outer) for i in range(1, outer)]
+
     barrier = pltpu.get_barrier_semaphore()
 
-    def greet(i, carry):
-        pl.semaphore_signal(
-            barrier, inc=1, device_id={"space": lax.rem(me + i, count)}, device_id_type=MESH
-        )
-        return carry
-
-    lax.fori_loop(1, count, greet, 0)
+    def greet(device):
+        pl.semaphore_signal(barrier, inc=1, device_id={"space": device}, device_id_type=MESH)
+
+    for d in range(4):
+        pl.when(sends[d])(functools.partial(greet, targets[d]))
+    for device in mates + peers:
+        greet(device)
+    greeted = len(mates) + len(peers) + sum(jnp.where(has, 1, 0) for has in receives)
 
     load_send.wait()
     load_x.wait()
@@ -80,7 +87,7 @@
         for j in range(capacity):
             outgoing[d, j] = x[send_in[d, j]]
         if d == 2:
-            pl.semaphore_wait(barrier, count - 1)
+            pl.semaphore_wait(barrier, greeted)
 
         @pl.when(sends[d])
         def _():
@@ -102,25 +109,35 @@
 
     right, right_t = doubled(tree), doubled(tree.T)
 
+    for load in loads:
+        load.wait()
+
     def prepare(c, carry):
         piece = pl.ds(c * part, part)
-        high, low = halves(x[piece])
+        own = x[piece]
+        extended[piece] = own
+        high, low = halves(own)
         paired = jnp.concatenate([high, low], 2)
         xs[piece] = paired
-        result = times(paired.reshape(part * nodes, 2 * species), right)
-        z[piece] = result.reshape(part, nodes, species)
+        weighted = times(paired.reshape(part * nodes, 2 * species), right)
+        weighted = weighted.reshape(part, nodes, species)
+        for i in range(part):
+            t = c * part + i
+            high, low = halves(tiles[t])
+            stacked = jnp.concatenate([high, low], 0)
+            a[t] = stacked
+            high, low = halves(weighted[i])
+            high_low = jnp.concatenate([high, low], 1)
+            both = lax.dot_general(
+                stacked,
+                jnp.concatenate([high_low, high_low], 0),
+                (((0,), (0,)), ((), ())),
+                preferred_element_type=jnp.float32,
+            )
+            pull[t] = (both[:, :species] + both[:, species:]).reshape(stored, nodes, species)
         return carry
 
     lax.fori_loop(0, CHUNKS, prepare, 0)
-    for load in loads:
-        load.wait()
-
-    def cut(t, carry):
-        high, low = halves(tiles[t])
-        a[t] = jnp.concatenate([high, low], 0)
-        return carry
-
-    lax.fori_loop(0, tile_rows, cut, 0, unroll=4)
     load_column.wait()
 
     for d in (0, 1, 2, 3):
@@ -128,62 +145,65 @@
         def _():
             copy_for(d).wait_recv()
             for j in range(capacity):
-                high, low = halves(received[d, j])
+                tile = received[d, j]
+                extended[tile_rows + d * capacity + j] = tile
+                high, low = halves(tile)
                 xs[tile_rows + d * capacity + j] = jnp.concatenate([high, low], 1)
 
-    def multiply(t, acc):
-        block = jnp.concatenate([xs[column_in[k, t]] for k in range(stored)], 0)
-        both = jnp.dot(a[t], block, preferred_element_type=jnp.float32)
-        small = both[:nodes, species:] + both[nodes:, :species] + both[nodes:, species:]
-        result = both[:nodes, :species] + small
-        spatial[t] = result
-        return acc + jnp.sum((z[t] * result).reshape(nodes // 8, 8, species), axis=0)
-
-    acc = lax.fori_loop(
-        0, tile_rows, multiply, jnp.zeros((8, species), jnp.float32), unroll=8
+    def weigh(t, acc):
+        for k in range(stored):
+            term = pull[t, k] * extended[column_in[k, t]]
+            acc = acc + jnp.sum(term.reshape(nodes // 8, 8, species), axis=0)
+        return acc
+
+    inner_shares[spot] = lax.fori_loop(
+        0, tile_rows, weigh, jnp.zeros((8, species), jnp.float32), unroll=4
     )
 
-    shares[me] = acc
-
-    def share_copy(i):
-        return pltpu.make_async_remote_copy(
-            src_ref=shares.at[me],
-            dst_ref=shares.at[me],
-            send_sem=share_send.at[i],
-            recv_sem=share_recv.at[i],
-            device_id={"space": lax.rem(me + i, count)},
-            device_id_type=MESH,
-        )
-
-    def give(i, carry):
-        share_copy(i).start()
-        return carry
-
-    lax.fori_loop(1, count, give, 0)
+    def share_copies(shares, mine, send, receive, devices):
+        return [
+            pltpu.make_async_remote_copy(
+                src_ref=shares.at[mine],
+                dst_ref=shares.at[mine],
+                send_sem=send.at[i],
+                recv_sem=receive.at[i],
+                device_id={"space": device},
+                device_id_type=MESH,
+            )
+            for i, device in enumerate(devices)
+        ]
+
+    first = share_copies(inner_shares, spot, inner_send, inner_recv, mates)
+    second = share_copies(outer_shares, team, outer_send, outer_recv, peers)
+    for copy in first:
+        copy.start()
 
     for c in range(CHUNKS):
-        piece = pl.ds(c * part, part)
-        high, low = halves(spatial[piece].reshape(part * nodes, species))
+        if c == CHUNKS // 2:
+            for copy in first:
+                copy.wait_recv()
+            outer_shares[team] = jnp.sum(inner_shares[...], axis=0)
+            for copy in second:
+                copy.start()
+        rows = []
+        for t in range(c * part, (c + 1) * part):
+            block = jnp.concatenate([xs[column_in[k, t]] for k in range(stored)], 0)
+            both = jnp.dot(a[t], block, preferred_element_type=jnp.float32)
+            small = both[:nodes, species:] + both[nodes:, :species] + both[nodes:, species:]
+            rows.append(both[:nodes, :species] + small)
+        high, low = halves(jnp.concatenate(rows, 0))
         result = times(jnp.concatenate([high, low], 1), right_t)
-        product_ref[piece] = result.reshape(part, nodes, species)
+        product_ref[pl.ds(c * part, part)] = result.reshape(part, nodes, species)
 
     for d in range(4):
         @pl.when(sends[d])
         def _():
             copy_for(d).wait_send()
-
-    def take(i, carry):
-        share_copy(i).wait_recv()
-        return carry
-
-    lax.fori_loop(1, count, take, 0)
-
-    def sent(i, carry):
-        share_copy(i).wait_send()
-        return carry
-
-    lax.fori_loop(1, count, sent, 0)
-    quad_ref[0] = jnp.sum(jnp.sum(shares[...], axis=0)) * scaling
+    for copy in second:
+        copy.wait_recv()
+    quad_ref[0] = jnp.sum(jnp.sum(outer_shares[...], axis=0)) * scaling
+    for copy in first + second:
+        copy.wait_send()
 
 
 def on_device(signal, space_tiles, tree_precision, send_tiles, column_tiles):
@@ -191,6 +211,8 @@
     tile_rows, nodes, width = space_tiles.shape
     species = signal.shape[1]
     directions, capacity = send_tiles.shape[1:]
+    stored = column_tiles.shape[1]
+    inner = max(i for i in range(1, math.isqrt(count) + 1) if count % i == 0)
     scaling = 1.0 / math.sqrt(count * tile_rows * nodes * species)
     vmem, f32, bf16 = pltpu.VMEM, jnp.float32, jnp.bfloat16
     dma = pltpu.SemaphoreType.DMA
@@ -211,18 +233,21 @@
             pltpu.SMEM(column_tiles.shape[::-1], jnp.int32),
             vmem((tile_rows, 2 * nodes, width), bf16),
             vmem((tile_rows + directions * capacity, nodes, 2 * species), bf16),
-            vmem(field, f32),
-            vmem(field, f32),
+            vmem((tile_rows + directions * capacity, nodes, species), f32),
+            vmem((tile_rows, stored, nodes, species), f32),
             vmem(lists, f32),
             vmem(lists, f32),
-            vmem((count, 8, species), f32),
+            vmem((inner, 8, species), f32),
+            vmem((count // inner, 8, species), f32),
             dma,
             dma((3,)),
             dma((CHUNKS,)),
             dma((directions,)),
             dma((directions,)),
-            dma((count,)),
-            dma((count,)),
+            dma((inner,)),
+            dma((inner,)),
+            dma((count // inner,)),
+            dma((count // inner,)),
         ],
         compiler_params=pltpu.CompilerParams(
             collective_id=0, has_side_effects=True, vmem_limit_bytes=40 * 2**20

time: 28.9 us -> 28.3 us (0.979)
  Pallas kernels: 25.4 us -> 24.8 us
    pallas_call x1, Pallas kernels: 25.4 us -> 24.8 us  [on_device(): pl.pallas_call(functools.partial(kernel, count, scaling), out_shape=(pltp...]
where the time goes in v3:
time: 28.3 us; the launch traced here: 28.1 us
  Pallas kernels  24.8 us (88%)
  between operations  2.33 us (8%)
  local copies, waits for them, and re-layouts  0.97 us (3%)
    pallas_call x1, Pallas kernels, on_device(): pl.pallas_call(functools.partial(kernel, count, scaling), out_shape=(pltp...  24.8 us
    unnamed x1, local copies, waits for them, and re-layouts  0.97 us

profile of v3, /device:TPU:0, one launch (start us, length us, event | category | flops | bytes accessed | tf_op | source)
XLA Modules:
  0.0 28.1 jit_solution(15998530261798145608)
XLA Ops:
  0.6 24.8 %kronecker_product.1 = (f32[32,64,128]{2,1,0:T(8,128)S(1)}, f32[1]{0:T(128)}) custom-call(f32[32,64,128]{2,1,0:T(8,128)} %bitcast.5, f32[32,64,384]{2,1,0:T(8,128)} %tiles_ref.1, f32[128,128]{1,0:T(8,128)} %tree_ref.1, s32[4,8]{1,0:T(4,128)} %bitcast.7, s32[6,32]{1,0:T(8,128)} %bitcast.6), custom_call_target="tpu_custom_call" | custom-call | flops 335544320 | bytes 5242880 | tf_op jit(solution)/shard_map/kronecker_product/pallas_call | solution.py:223
  25.4 1.0 %copy.9 = f32[2048,128]{1,0:T(8,128)} copy(f32[2048,128]{1,0:T(8,128)S(1)} %bitcast.4) | data formatting | bytes 2097152

commit v4 on v2

v4 whole, which is shorter than its diff:
```python
import functools
import math

import jax
import jax.numpy as jnp
from jax import lax
from jax.experimental import pallas as pl
from jax.experimental.pallas import tpu as pltpu
from jax.sharding import PartitionSpec as P

ROWS = 8
CHUNKS = 4
GROUP = 4
MESH = pl.DeviceIdType.MESH


def halves(value):
    high = value.astype(jnp.bfloat16)
    low = (value - high.astype(jnp.float32)).astype(jnp.bfloat16)
    return high, low


def doubled(matrix):
    high, low = halves(matrix)
    zero = jnp.zeros_like(low)
    return jnp.concatenate(
        [jnp.concatenate([high, low], 1), jnp.concatenate([high, zero], 1)], 0
    )


def times(paired, weights):
    both = jnp.dot(paired, weights, preferred_element_type=jnp.float32)
    half = both.shape[1] // 2
    return both[:, :half] + both[:, half:]


def tile_product(stacked, block):
    both = jnp.dot(stacked, block, preferred_element_type=jnp.float32)
    nodes, species = both.shape[0] // 2, both.shape[1] // 2
    small = both[:nodes, species:] + both[nodes:, :species] + both[nodes:, species:]
    return both[:nodes, :species] + small


def rows_product(stacked, columns, xs, z, weights):
    rows, shares = [], []
    for t, row_columns in enumerate(columns):
        block = jnp.concatenate([xs[c] for c in row_columns], 0)
        rows.append(tile_product(stacked[t], block))
        term = z[t] * rows[-1]
        shares.append(jnp.sum(term.reshape(-1, 8, term.shape[-1]), axis=0))
    high, low = halves(jnp.concatenate(rows, 0))
    result = times(jnp.concatenate([high, low], 1), weights)
    return result.reshape(len(rows), -1, result.shape[-1]), shares


def send_and_interior(
    count,
    signal_ref, tiles_ref, tree_ref, send_ref, column_ref,
    product, xs, a, z, shares, weights,
    x, tiles, tree_in, send_in, column_in, outgoing, received,
    x_sem, small_sem, tiles_sem, send_sem, recv_sem,
):
    tile_rows, nodes, species = x.shape
    stored = column_ref.shape[0]
    capacity = send_ref.shape[1]
    load_send = pltpu.make_async_copy(send_ref, send_in, small_sem.at[0])
    load_send.start()
    load_x = pltpu.make_async_copy(signal_ref, x, x_sem)
    load_x.start()
    load_tree = pltpu.make_async_copy(tree_ref, tree_in, small_sem.at[1])
    load_tree.start()
    load_column = pltpu.make_async_copy(column_ref, column_in, small_sem.at[2])
    load_column.start()
    wide = count // ROWS
    me = lax.axis_index("space")
    column, row = lax.rem(me, wide), me // wide
    not_first, not_last = column > 0, column < wide - 1
    above, below = row > 0, row < ROWS - 1
    sends = (not_last, not_first, below, above)
    receives = (not_first, not_last, above, below)
    targets = (me + 1, me - 1, me + wide, me - wide)

    part = tile_rows // CHUNKS
    loads = []
    for c in range(CHUNKS):
        piece = pl.ds(c * part, part)
        loads.append(pltpu.make_async_copy(tiles_ref.at[piece], tiles.at[piece], tiles_sem.at[c]))
        loads[-1].start()

    barrier = pltpu.get_barrier_semaphore()

    def greet(device):
        pl.semaphore_signal(barrier, inc=1, device_id={"space": device}, device_id_type=MESH)

    for d in range(4):
        pl.when(sends[d])(functools.partial(greet, targets[d]))
    greeted = sum(jnp.where(has, 1, 0) for has in receives)

    load_send.wait()
    load_x.wait()

    def copy_for(d):
        return pltpu.make_async_remote_copy(
            src_ref=outgoing.at[d],
            dst_ref=received.at[d],
            send_sem=send_sem.at[d],
            recv_sem=recv_sem.at[d],
            device_id={"space": targets[d]},
            device_id_type=MESH,
        )

    for d in (2, 3, 0, 1):
        for j in range(capacity):
            outgoing[d, j] = x[send_in[d, j]]
        if d == 2:
            pl.semaphore_wait(barrier, greeted)

        @pl.when(sends[d])
        def _():
            copy_for(d).start()

    load_tree.wait()
    tree = tree_in[...]
    right, right_t = doubled(tree), doubled(tree.T)

    weights[...] = right_t
    load_column.wait()

    def prepare(c, carry):
        piece = pl.ds(c * part, part)
        high, low = halves(x[piece])
        paired = jnp.concatenate([high, low], 2)
        xs[piece] = paired
        weighted = times(paired.reshape(part * nodes, 2 * species), right)
        z[piece] = weighted.reshape(part, nodes, species)
        return carry

    lax.fori_loop(0, CHUNKS, prepare, 0)
    for load in loads:
        load.wait()

    def interior(c, carry):
        first = c * part
        piece = pl.ds(first, part)
        high, low = halves(tiles[piece])
        a[piece] = jnp.concatenate([high, low], 1)
        own = [
            [jnp.minimum(column_in[k, first + t], tile_rows - 1) for k in range(stored)]
            for t in range(part)
        ]
        result, sums = rows_product(a.at[piece], own, xs, z.at[piece], right_t)
        product[piece] = result
        for t in range(part):
            shares[first + t] = sums[t]
        return carry

    lax.fori_loop(0, CHUNKS, interior, 0)

    for d in (0, 1, 2, 3):
        @pl.when(receives[d])
        def _():
            copy_for(d).wait_recv()
            for j in range(capacity):
                high, low = halves(received[d, j])
                xs[tile_rows + d * capacity + j] = jnp.concatenate([high, low], 1)
    for d in range(4):
        @pl.when(sends[d])
        def _():
            copy_for(d).wait_send()


def boundary(
    interior, xs, a, z, shares, weights, columns_ref, product_ref, total_ref,
    again, columns, column_sem, out_sem,
):
    tile_rows = interior.shape[0]
    stored = columns.shape[0]
    load = pltpu.make_async_copy(columns_ref, columns, column_sem)
    load.start()
    load.wait()

    def group(g, acc):
        first = g * GROUP
        piece = pl.ds(first, GROUP)
        named = [[columns[k, first + t] for k in range(stored)] for t in range(GROUP)]
        furthest = functools.reduce(jnp.maximum, [c for row in named for c in row])

        def compute():
            result, sums = rows_product(a.at[piece], named, xs, z.at[piece], weights[...])
            again[piece] = result
            pltpu.make_async_copy(again.at[piece], product_ref.at[piece], out_sem).start()
            return functools.reduce(jnp.add, sums)

        def keep():
            pltpu.make_async_copy(interior.at[piece], product_ref.at[piece], out_sem).start()
            return jnp.sum(shares[piece], axis=0)

        return acc + lax.cond(furthest >= tile_rows, compute, keep)

    total_ref[...] = lax.fori_loop(0, tile_rows // GROUP, group, jnp.zeros_like(total_ref))
    pltpu.make_async_copy(again, product_ref, out_sem).wait()


def sum_shares(
    scaling, total_ref, quad_ref,
    inner_shares, outer_shares, inner_send, inner_recv, outer_send, outer_recv,
):
    me = lax.axis_index("space")
    inner, outer = inner_shares.shape[0], outer_shares.shape[0]
    spot, team = lax.rem(me, inner), me // inner
    mates = [team * inner + lax.rem(spot + i, inner) for i in range(1, inner)]
    peers = [spot + inner * lax.rem(team + i, outer) for i in range(1, outer)]

    barrier = pltpu.get_barrier_semaphore()
    for device in mates + peers:
        pl.semaphore_signal(barrier, inc=1, device_id={"space": device}, device_id_type=MESH)

    def share_copies(shares, mine, send, receive, devices):
        return [
            pltpu.make_async_remote_copy(
                src_ref=shares.at[mine],
                dst_ref=shares.at[mine],
                send_sem=send.at[i],
                recv_sem=receive.at[i],
                device_id={"space": device},
                device_id_type=MESH,
            )
            for i, device in enumerate(devices)
        ]

    first = share_copies(inner_shares, spot, inner_send, inner_recv, mates)
    second = share_copies(outer_shares, team, outer_send, outer_recv, peers)
    inner_shares[spot] = total_ref[...]
    pl.semaphore_wait(barrier, len(mates) + len(peers))
    for copy in first:
        copy.start()
    for copy in first:
        copy.wait_recv()
    outer_shares[team] = jnp.sum(inner_shares[...], axis=0)
    for copy in second:
        copy.start()
    for copy in second:
        copy.wait_recv()
    quad_ref[0] = jnp.sum(jnp.sum(outer_shares[...], axis=0)) * scaling
    for copy in first + second:
        copy.wait_send()


def on_device(signal, space_tiles, tree_precision, send_tiles, column_tiles):
    count = lax.axis_size("space")
    tile_rows, nodes, width = space_tiles.shape
    stored = column_tiles.shape[1]
    species = signal.shape[1]
    directions, capacity = send_tiles.shape[1:]
    inner = max(i for i in range(1, math.isqrt(count) + 1) if count % i == 0)
    scaling = 1.0 / math.sqrt(count * tile_rows * nodes * species)
    vmem, f32, bf16 = pltpu.VMEM, jnp.float32, jnp.bfloat16
    dma = pltpu.SemaphoreType.DMA
    hbm = pl.BlockSpec(memory_space=pltpu.HBM)
    near = pl.BlockSpec(memory_space=vmem)
    smem = pl.BlockSpec(memory_space=pltpu.SMEM)
    field = (tile_rows, nodes, species)
    lists = (directions, capacity, nodes, species)
    share = (8, species)
    columns = column_tiles.T
    flops = 2 * tile_rows * nodes * species * (width + 2 * species)
    between = (
        vmem(field, f32),
        vmem((tile_rows + directions * capacity, nodes, 2 * species), bf16),
        vmem((tile_rows, 2 * nodes, width), bf16),
        vmem(field, f32),
        vmem((tile_rows, *share), f32),
        vmem((2 * species, 2 * species), bf16),
    )
    kept = pl.pallas_call(
        functools.partial(send_and_interior, count),
        out_shape=between,
        in_specs=[hbm] * 5,
        out_specs=(near,) * len(between),
        scratch_shapes=[
            vmem(field, f32),
            vmem(space_tiles.shape, f32),
            vmem(tree_precision.shape, f32),
            pltpu.SMEM((directions, capacity), jnp.int32),
            pltpu.SMEM(columns.shape, jnp.int32),
            vmem(lists, f32),
            vmem(lists, f32),
            dma,
            dma((3,)),
            dma((CHUNKS,)),
            dma((directions,)),
            dma((directions,)),
        ],
        compiler_params=pltpu.CompilerParams(
            collective_id=0, has_side_effects=True, vmem_limit_bytes=24 * 2**20
        ),
        cost_estimate=pl.CostEstimate(
            flops=flops, bytes_accessed=4 * (space_tiles.size + signal.size), transcendentals=0
        ),
        name="send_and_interior",
    )(*(
        pltpu.with_memory_space_constraint(array, pltpu.HBM)
        for array in (signal.reshape(field), space_tiles, tree_precision, send_tiles[0], columns)
    ))
    product, total = pl.pallas_call(
        boundary,
        out_shape=(jax.ShapeDtypeStruct(field, f32), vmem(share, f32)),
        in_specs=[near] * len(between) + [hbm],
        out_specs=(hbm, near),
        scratch_shapes=[vmem(field, f32), pltpu.SMEM(columns.shape, jnp.int32), dma, dma],
        compiler_params=pltpu.CompilerParams(vmem_limit_bytes=16 * 2**20),
        cost_estimate=pl.CostEstimate(
            flops=flops, bytes_accessed=4 * signal.size, transcendentals=0
        ),
        name="boundary",
    )(*kept, pltpu.with_memory_space_constraint(columns, pltpu.HBM))
    quad = pl.pallas_call(
        functools.partial(sum_shares, scaling),
        out_shape=jax.ShapeDtypeStruct((1,), f32),
        in_specs=[near],
        out_specs=smem,
        scratch_shapes=[
            vmem((inner, *share), f32),
            vmem((count // inner, *share), f32),
            dma((inner,)),
            dma((inner,)),
            dma((count // inner,)),
            dma((count // inner,)),
        ],
        compiler_params=pltpu.CompilerParams(collective_id=1, has_side_effects=True),
        name="sum_shares",
    )(total)
    return product.reshape(signal.shape), quad


def solution(mesh):
    placed = (
        P(("groups", "space"), None),
        P("space", None, None),
        P("groups", None),
        P("space", None, None),
        P("space", None),
    )
    return jax.shard_map(
        on_device,
        mesh=mesh,
        in_specs=placed,
        out_specs=(P(("groups", "space"), None), P("groups")),
        check_vma=False,
    )
```

time: 28.9 us -> 33.1 us (1.15)
  Pallas kernels: 25.4 us -> 29.9 us
  local copies, waits for them, and re-layouts: 0.97 us -> 0.58 us
    pallas_call x1 -> x3, Pallas kernels: 25.4 us -> 29.9 us  [the longest x1 14.4 us: on_device(): pl.pallas_call(functools.partial(send_and_interior, count), out_shape=bet...]
    unnamed x1 -> x2, local copies, waits for them, and re-layouts: 0.97 us -> 0.58 us
where the time goes in v4:
time: 33.1 us; the launch traced here: 32.9 us
  Pallas kernels  29.9 us (90%)
  between operations  2.39 us (7%)
  local copies, waits for them, and re-layouts  0.58 us (2%)
    pallas_call x1, Pallas kernels, on_device(): pl.pallas_call(functools.partial(send_and_interior, count), out_shape=bet...  14.4 us
    pallas_call x1, Pallas kernels, on_device(): pl.pallas_call(functools.partial(sum_shares, scaling), out_shape=jax.Shap...  12.8 us
    pallas_call x1, Pallas kernels, on_device(): pl.pallas_call(boundary, out_shape=(jax.ShapeDtypeStruct(field, f32), vme...  2.73 us

profile of v4, /device:TPU:0, one launch (start us, length us, event | category | flops | bytes accessed | tf_op | source)
XLA Modules:
  0.0 32.9 jit_solution(8157942769538908156)
XLA Ops:
  0.6 14.4 %send_and_interior.1 = (f32[32,64,128]{2,1,0:T(8,128)S(1)}, bf16[64,64,256]{2,1,0:T(8,128)(2,1)S(1)}, bf16[32,128,384]{2,1,0:T(8,128)(2,1)S(1)}, f32[32,64,128]{...) custom-call(f32[32,64,128]{2,1,0:T(8,128)} %bitcast.4, f32[32,64,384]{2,1,0:T(8,128)} %tiles_ref.1, ...), custom_call_target="tpu_custom_call" | custom-call | flops 335544320 | bytes 4194304 | tf_op jit(solution)/shard_map/send_and_interior/pallas_call | solution.py:275
  15.0 2.7 %boundary.1 = (f32[32,64,128]{2,1,0:T(8,128)}, f32[8,128]{1,0:T(8,128)S(1)}) custom-call(f32[32,64,128]{2,1,0:T(8,128)S(1)} %get-tuple-element.10.interior, bf16[64,64,256]{2,1,0:T(8,128)(2,1)S(1)} %get-tuple-element.11.xs, bf16[32,128,384]{2,1,0:T(8,128)(2,1)S(1)} %get-tuple-element.12.a, f32[32,64,128]{2,1,0:T(8,128)S(1)} %get-tuple-element.13.z, ...), custom_call_target="tpu_custom_call" | custom-call | flops 335544320 | bytes 1048576 | tf_op jit(solution)/shard_map/boundary/pallas_call | solution.py:305
  17.8 0.0 copy-start
  17.8 0.6 %copy-done = f32[8,128]{1,0:T(8,128)} copy-done((f32[8,128]{1,0:T(8,128)}, f32[8,128]{1,0:T(8,128)S(1)}, u32[]{:S(2)}) %copy-start) | copy-done | bytes 4120
  18.3 12.8 %sum_shares.1 = f32[1]{0:T(128)} custom-call(f32[8,128]{1,0:T(8,128)} %copy-done), custom_call_target="tpu_custom_call" | custom-call | tf_op jit(solution)/shard_map/sum_shares/pallas_call | solution.py:317
Async XLA Ops:
  17.8 0.6 %copy-start = (f32[8,128]{1,0:T(8,128)}, f32[8,128]{1,0:T(8,128)S(1)}, u32[]{:S(2)}) copy-start(f32[8,128]{1,0:T(8,128)S(1)} %get-tuple-element.17.total_ref) | copy-start | bytes 12292

commit v5 on v3

v5 whole, which is shorter than its diff:
```python
import functools
import math

import jax
import jax.numpy as jnp
from jax import lax
from jax.experimental import pallas as pl
from jax.experimental.pallas import tpu as pltpu
from jax.sharding import PartitionSpec as P

ROWS = 8
CHUNKS = 4
GROUP = 4
MESH = pl.DeviceIdType.MESH


def halves(value):
    high = value.astype(jnp.bfloat16)
    low = (value - high.astype(jnp.float32)).astype(jnp.bfloat16)
    return high, low


def doubled(matrix):
    high, low = halves(matrix)
    zero = jnp.zeros_like(low)
    return jnp.concatenate(
        [jnp.concatenate([high, low], 1), jnp.concatenate([high, zero], 1)], 0
    )


def times(paired, weights):
    both = jnp.dot(paired, weights, preferred_element_type=jnp.float32)
    half = both.shape[1] // 2
    return both[:, :half] + both[:, half:]


def tile_product(stacked, block):
    both = jnp.dot(stacked, block, preferred_element_type=jnp.float32)
    nodes, species = both.shape[0] // 2, both.shape[1] // 2
    small = both[:nodes, species:] + both[nodes:, :species] + both[nodes:, species:]
    return both[:nodes, :species] + small


def rows_product(stacked, columns, xs, weights):
    rows = []
    for t, row_columns in enumerate(columns):
        block = jnp.concatenate([xs[c] for c in row_columns], 0)
        rows.append(tile_product(stacked[t], block))
    high, low = halves(jnp.concatenate(rows, 0))
    result = times(jnp.concatenate([high, low], 1), weights)
    return result.reshape(len(rows), -1, result.shape[-1])


def send_and_interior(
    count, scaling,
    signal_ref, tiles_ref, tree_ref, send_ref, column_ref,
    product, xs, a, weights, quad_ref,
    x, tiles, tree_in, send_in, column_in, extended, pull, outgoing, received, shares,
    x_sem, small_sem, tiles_sem, send_sem, recv_sem, share_send, share_recv,
):
    tile_rows, nodes, species = x.shape
    stored = column_ref.shape[0]
    capacity = send_ref.shape[1]
    load_send = pltpu.make_async_copy(send_ref, send_in, small_sem.at[0])
    load_send.start()
    load_x = pltpu.make_async_copy(signal_ref, x, x_sem)
    load_x.start()
    load_tree = pltpu.make_async_copy(tree_ref, tree_in, small_sem.at[1])
    load_tree.start()
    load_column = pltpu.make_async_copy(column_ref, column_in, small_sem.at[2])
    load_column.start()
    wide = count // ROWS
    me = lax.axis_index("space")
    column, row = lax.rem(me, wide), me // wide
    not_first, not_last = column > 0, column < wide - 1
    above, below = row > 0, row < ROWS - 1
    sends = (not_last, not_first, below, above)
    receives = (not_first, not_last, above, below)
    targets = (me + 1, me - 1, me + wide, me - wide)

    part = tile_rows // CHUNKS
    loads = []
    for c in range(CHUNKS):
        piece = pl.ds(c * part, part)
        loads.append(pltpu.make_async_copy(tiles_ref.at[piece], tiles.at[piece], tiles_sem.at[c]))
        loads[-1].start()

    barrier = pltpu.get_barrier_semaphore()

    others = [lax.rem(me + i, count) for i in range(1, count)]
    for device in others:
        pl.semaphore_signal(barrier, inc=1, device_id={"space": device}, device_id_type=MESH)

    load_send.wait()
    load_x.wait()

    def copy_for(d):
        return pltpu.make_async_remote_copy(
            src_ref=outgoing.at[d],
            dst_ref=received.at[d],
            send_sem=send_sem.at[d],
            recv_sem=recv_sem.at[d],
            device_id={"space": targets[d]},
            device_id_type=MESH,
        )

    for d in (2, 3, 0, 1):
        for j in range(capacity):
            outgoing[d, j] = x[send_in[d, j]]
        if d == 2:
            pl.semaphore_wait(barrier, count - 1)

        @pl.when(sends[d])
        def _():
            copy_for(d).start()

    load_tree.wait()
    tree = tree_in[...]
    right, right_t = doubled(tree), doubled(tree.T)

    weights[...] = right_t
    load_column.wait()

    for load in loads:
        load.wait()

    def prepare(c, carry):
        piece = pl.ds(c * part, part)
        own = x[piece]
        extended[piece] = own
        high, low = halves(own)
        paired = jnp.concatenate([high, low], 2)
        xs[piece] = paired
        weighted = times(paired.reshape(part * nodes, 2 * species), right)
        weighted = weighted.reshape(part, nodes, species)
        for i in range(part):
            t = c * part + i
            high, low = halves(tiles[t])
            stacked = jnp.concatenate([high, low], 0)
            a[t] = stacked
            high, low = halves(weighted[i])
            high_low = jnp.concatenate([high, low], 1)
            both = lax.dot_general(
                stacked,
                jnp.concatenate([high_low, high_low], 0),
                (((0,), (0,)), ((), ())),
                preferred_element_type=jnp.float32,
            )
            pull[t] = (both[:, :species] + both[:, species:]).reshape(stored, nodes, species)
        return carry

    lax.fori_loop(0, CHUNKS, prepare, 0)

    def multiply(c, last):
        first = c * part
        piece = pl.ds(first, part)
        named = [
            [jnp.minimum(column_in[k, first + t], last) for k in range(stored)]
            for t in range(part)
        ]
        product[piece] = rows_product(a.at[piece], named, xs, right_t)

    def interior(c, carry):
        multiply(c, tile_rows - 1)
        return carry

    lax.fori_loop(CHUNKS // 2, CHUNKS, interior, 0)

    for d in (0, 1, 2, 3):
        @pl.when(receives[d])
        def _():
            copy_for(d).wait_recv()
            for j in range(capacity):
                tile = received[d, j]
                extended[tile_rows + d * capacity + j] = tile
                high, low = halves(tile)
                xs[tile_rows + d * capacity + j] = jnp.concatenate([high, low], 1)

    def weigh(t, acc):
        for k in range(stored):
            term = pull[t, k] * extended[column_in[k, t]]
            acc = acc + jnp.sum(term.reshape(nodes // 8, 8, species), axis=0)
        return acc

    shares[me] = lax.fori_loop(
        0, tile_rows, weigh, jnp.zeros((8, species), jnp.float32), unroll=4
    )
    copies = [
        pltpu.make_async_remote_copy(
            src_ref=shares.at[me],
            dst_ref=shares.at[me],
            send_sem=share_send.at[i],
            recv_sem=share_recv.at[i],
            device_id={"space": device},
            device_id_type=MESH,
        )
        for i, device in enumerate(others)
    ]
    for copy in copies:
        copy.start()

    def full(c, carry):
        multiply(c, xs.shape[0] - 1)
        return carry

    lax.fori_loop(0, CHUNKS // 2, full, 0)

    for d in range(4):
        @pl.when(sends[d])
        def _():
            copy_for(d).wait_send()
    for copy in copies:
        copy.wait_recv()
    quad_ref[0] = jnp.sum(jnp.sum(shares[...], axis=0)) * scaling
    for copy in copies:
        copy.wait_send()


def boundary(
    done, interior, xs, a, weights, columns_ref, product_ref, again, columns, column_sem, out_sem,
):
    tile_rows = interior.shape[0]
    stored = columns.shape[0]
    load = pltpu.make_async_copy(columns_ref, columns, column_sem)
    load.start()
    final = pl.ds(0, done)
    pltpu.make_async_copy(interior.at[final], product_ref.at[final], out_sem).start()
    load.wait()

    def group(g, carry):
        first = g * GROUP
        piece = pl.ds(first, GROUP)
        named = [[columns[k, first + t] for k in range(stored)] for t in range(GROUP)]
        furthest = functools.reduce(jnp.maximum, [c for row in named for c in row])

        @pl.when(furthest >= tile_rows)
        def _():
            again[piece] = rows_product(a.at[piece], named, xs, weights[...])
            pltpu.make_async_copy(again.at[piece], product_ref.at[piece], out_sem).start()

        @pl.when(furthest < tile_rows)
        def _():
            pltpu.make_async_copy(interior.at[piece], product_ref.at[piece], out_sem).start()

        return carry

    lax.fori_loop(done // GROUP, tile_rows // GROUP, group, 0)
    pltpu.make_async_copy(again, product_ref, out_sem).wait()


def on_device(signal, space_tiles, tree_precision, send_tiles, column_tiles):
    count = lax.axis_size("space")
    tile_rows, nodes, width = space_tiles.shape
    stored = column_tiles.shape[1]
    species = signal.shape[1]
    directions, capacity = send_tiles.shape[1:]
    scaling = 1.0 / math.sqrt(count * tile_rows * nodes * species)
    vmem, f32, bf16 = pltpu.VMEM, jnp.float32, jnp.bfloat16
    dma = pltpu.SemaphoreType.DMA
    hbm = pl.BlockSpec(memory_space=pltpu.HBM)
    near = pl.BlockSpec(memory_space=vmem)
    smem = pl.BlockSpec(memory_space=pltpu.SMEM)
    field = (tile_rows, nodes, species)
    lists = (directions, capacity, nodes, species)
    columns = column_tiles.T
    flops = 2 * tile_rows * nodes * species * (width + 2 * species)
    between = (
        vmem(field, f32),
        vmem((tile_rows + directions * capacity, nodes, 2 * species), bf16),
        vmem((tile_rows, 2 * nodes, width), bf16),
        vmem((2 * species, 2 * species), bf16),
    )
    *kept, quad = pl.pallas_call(
        functools.partial(send_and_interior, count, scaling),
        out_shape=(*between, jax.ShapeDtypeStruct((1,), f32)),
        in_specs=[hbm] * 5,
        out_specs=(near,) * len(between) + (smem,),
        scratch_shapes=[
            vmem(field, f32),
            vmem(space_tiles.shape, f32),
            vmem(tree_precision.shape, f32),
            pltpu.SMEM((directions, capacity), jnp.int32),
            pltpu.SMEM(columns.shape, jnp.int32),
            vmem((tile_rows + directions * capacity, nodes, species), f32),
            vmem((tile_rows, stored, nodes, species), f32),
            vmem(lists, f32),
            vmem(lists, f32),
            vmem((count, 8, species), f32),
            dma,
            dma((3,)),
            dma((CHUNKS,)),
            dma((directions,)),
            dma((directions,)),
            dma((count,)),
            dma((count,)),
        ],
        compiler_params=pltpu.CompilerParams(
            collective_id=0, has_side_effects=True, vmem_limit_bytes=32 * 2**20
        ),
        cost_estimate=pl.CostEstimate(
            flops=flops, bytes_accessed=4 * (space_tiles.size + signal.size), transcendentals=0
        ),
        name="send_and_interior",
    )(*(
        pltpu.with_memory_space_constraint(array, pltpu.HBM)
        for array in (signal.reshape(field), space_tiles, tree_precision, send_tiles[0], columns)
    ))
    product = pl.pallas_call(
        functools.partial(boundary, tile_rows // CHUNKS * (CHUNKS // 2)),
        out_shape=jax.ShapeDtypeStruct(field, f32),
        in_specs=[near] * len(between) + [hbm],
        out_specs=hbm,
        scratch_shapes=[vmem(field, f32), pltpu.SMEM(columns.shape, jnp.int32), dma, dma],
        compiler_params=pltpu.CompilerParams(vmem_limit_bytes=16 * 2**20),
        cost_estimate=pl.CostEstimate(
            flops=flops, bytes_accessed=4 * signal.size, transcendentals=0
        ),
        name="boundary",
    )(*kept, pltpu.with_memory_space_constraint(columns, pltpu.HBM))
    return product.reshape(signal.shape), quad


def solution(mesh):
    placed = (
        P(("groups", "space"), None),
        P("space", None, None),
        P("groups", None),
        P("space", None, None),
        P("space", None),
    )
    return jax.shard_map(
        on_device,
        mesh=mesh,
        in_specs=placed,
        out_specs=(P(("groups", "space"), None), P("groups")),
        check_vma=False,
    )
```

time: 28.3 us -> 28.2 us (level)
  local copies, waits for them, and re-layouts: 0.97 us -> 0 us
  Pallas kernels: 24.8 us -> 25.7 us
    unnamed x1 -> x0, local copies, waits for them, and re-layouts: 0.97 us -> none
    pallas_call x1 -> x2, Pallas kernels: 24.8 us -> 25.7 us  [the longest x1 24.1 us: on_device(): pl.pallas_call(functools.partial(send_and_interior, count, scaling), out_...]
where the time goes in v5:
time: 28.2 us; the launch traced here: 28 us
  Pallas kernels  25.7 us (91%)
  between operations  2.33 us (8%)
    pallas_call x1, Pallas kernels, on_device(): pl.pallas_call(functools.partial(send_and_interior, count, scaling), out_...  24.1 us
    pallas_call x1, Pallas kernels, on_device(): pl.pallas_call(functools.partial(boundary, tile_rows // CHUNKS * (CHUNKS...  1.59 us

profile of v5, /device:TPU:0, one launch (start us, length us, event | category | flops | bytes accessed | tf_op | source)
XLA Modules:
  0.0 28.0 jit_solution(10364681208291624789)
XLA Ops:
  0.6 24.1 %send_and_interior.1 = (f32[32,64,128]{2,1,0:T(8,128)S(1)}, bf16[64,64,256]{2,1,0:T(8,128)(2,1)S(1)}, bf16[32,128,384]{2,1,0:T(8,128)(2,1)S(1)}, bf16[256,256]{1,0:T(8,128)(2,1)S(1)}, f32[1]{0:T(128)}) custom-call(f32[32,64,128]{2,1,0:T(8,128)} %bitcast.4, f32[32,64,384]{2,1,0:T(8,128)} %tiles_ref.1, f32[128,128]{1,0:T(8,128)} %tree_ref.1, s32[4,8]{1,0:T(4,128)} %bitcast.8, ...), custom_call_target="tpu_custom_call" | custom-call | flops 335544320 | bytes 4194304 | tf_op jit(solution)/shard_map/send_and_interior/pallas_call | solution.py:273
  24.7 1.6 %boundary.1 = f32[32,64,128]{2,1,0:T(8,128)} custom-call(f32[32,64,128]{2,1,0:T(8,128)S(1)} %get-tuple-element.7.interior, bf16[64,64,256]{2,1,0:T(8,128)(2,1)S(1)} %get-tuple-element.8.xs, bf16[32,128,384]{2,1,0:T(8,128)(2,1)S(1)} %get-tuple-element.9.a, bf16[256,256]{1,0:T(8,128)(2,1)S(1)} %get-tuple-element.10.weights, s32[6,32]{1,0:T(8,128)} %bitcast.7), custom_call_target="tpu_custom_call" | custom-call | flops 335544320 | bytes 1048576 | tf_op jit(solution)/shard_map/boundary/pallas_call | solution.py:308

commit v6 on v5

--- a/solution.py
+++ b/solution.py
@@ -10,6 +10,7 @@
 
 ROWS = 8
 CHUNKS = 4
+FULL = 3
 GROUP = 4
 MESH = pl.DeviceIdType.MESH
 
@@ -25,6 +26,13 @@
     zero = jnp.zeros_like(low)
     return jnp.concatenate(
         [jnp.concatenate([high, low], 1), jnp.concatenate([high, zero], 1)], 0
+    )
+
+
+def apart(one, two):
+    zero = jnp.zeros_like(one)
+    return jnp.concatenate(
+        [jnp.concatenate([one, zero], 1), jnp.concatenate([zero, two], 1)], 0
     )
 
 
@@ -133,20 +141,25 @@
         xs[piece] = paired
         weighted = times(paired.reshape(part * nodes, 2 * species), right)
         weighted = weighted.reshape(part, nodes, species)
+        z_high, z_low = halves(weighted)
         for i in range(part):
             t = c * part + i
             high, low = halves(tiles[t])
-            stacked = jnp.concatenate([high, low], 0)
-            a[t] = stacked
-            high, low = halves(weighted[i])
-            high_low = jnp.concatenate([high, low], 1)
-            both = lax.dot_general(
-                stacked,
-                jnp.concatenate([high_low, high_low], 0),
-                (((0,), (0,)), ((), ())),
+            a[t] = jnp.concatenate([high, low], 0)
+        for i in range(0, part, 2):
+            t = c * part + i
+            turned = tiles[pl.ds(t, 2)].reshape(2 * nodes, stored * nodes).T
+            high, low = halves(turned)
+            both = jnp.dot(
+                jnp.concatenate([high, low, high], 1),
+                jnp.concatenate(
+                    [apart(z_high[i], z_high[i + 1])] * 2 + [apart(z_low[i], z_low[i + 1])], 0
+                ),
                 preferred_element_type=jnp.float32,
             )
-            pull[t] = (both[:, :species] + both[:, species:]).reshape(stored, nodes, species)
+            for j in range(2):
+                mine = both[:, j * species : (j + 1) * species]
+                pull[t + j] = mine.reshape(stored, nodes, species)
         return carry
 
     lax.fori_loop(0, CHUNKS, prepare, 0)
@@ -164,7 +177,7 @@
         multiply(c, tile_rows - 1)
         return carry
 
-    lax.fori_loop(CHUNKS // 2, CHUNKS, interior, 0)
+    lax.fori_loop(FULL, CHUNKS, interior, 0)
 
     for d in (0, 1, 2, 3):
         @pl.when(receives[d])
@@ -203,7 +216,7 @@
         multiply(c, xs.shape[0] - 1)
         return carry
 
-    lax.fori_loop(0, CHUNKS // 2, full, 0)
+    lax.fori_loop(0, FULL, full, 0)
 
     for d in range(4):
         @pl.when(sends[d])
@@ -306,7 +319,7 @@
         for array in (signal.reshape(field), space_tiles, tree_precision, send_tiles[0], columns)
     ))
     product = pl.pallas_call(
-        functools.partial(boundary, tile_rows // CHUNKS * (CHUNKS // 2)),
+        functools.partial(boundary, tile_rows // CHUNKS * FULL),
         out_shape=jax.ShapeDtypeStruct(field, f32),
         in_specs=[near] * len(between) + [hbm],
         out_specs=hbm,

time: 28.2 us -> 28.1 us (level)
  no operation moved by 1% of the time
where the time goes in v6:
time: 28.1 us; the launch traced here: 27.9 us
  Pallas kernels  25.6 us (91%)
  between operations  2.33 us (8%)
    pallas_call x1, Pallas kernels, on_device(): pl.pallas_call(functools.partial(send_and_interior, count, scaling), out_...  24.1 us
    pallas_call x1, Pallas kernels, on_device(): pl.pallas_call(functools.partial(boundary, tile_rows // CHUNKS * FULL), o...  1.49 us

profile of v6, /device:TPU:0, one launch (start us, length us, event | category | flops | bytes accessed | tf_op | source)
XLA Modules:
  0.0 27.9 jit_solution(12549356114112531747)
XLA Ops:
  0.6 24.1 %send_and_interior.1 = (f32[32,64,128]{2,1,0:T(8,128)S(1)}, bf16[64,64,256]{2,1,0:T(8,128)(2,1)S(1)}, bf16[32,128,384]{2,1,0:T(8,128)(2,1)S(1)}, bf16[256,256]{1,0:T(8,128)(2,1)S(1)}, f32[1]{0:T(128)}) custom-call(f32[32,64,128]{2,1,0:T(8,128)} %bitcast.4, f32[32,64,384]{2,1,0:T(8,128)} %tiles_ref.1, f32[128,128]{1,0:T(8,128)} %tree_ref.1, s32[4,8]{1,0:T(4,128)} %bitcast.8, ...), custom_call_target="tpu_custom_call" | custom-call | flops 335544320 | bytes 4194304 | tf_op jit(solution)/shard_map/send_and_interior/pallas_call | solution.py:286
  24.7 1.5 %boundary.1 = f32[32,64,128]{2,1,0:T(8,128)} custom-call(f32[32,64,128]{2,1,0:T(8,128)S(1)} %get-tuple-element.7.interior, bf16[64,64,256]{2,1,0:T(8,128)(2,1)S(1)} %get-tuple-element.8.xs, bf16[32,128,384]{2,1,0:T(8,128)(2,1)S(1)} %get-tuple-element.9.a, bf16[256,256]{1,0:T(8,128)(2,1)S(1)} %get-tuple-element.10.weights, s32[6,32]{1,0:T(8,128)} %bitcast.7), custom_call_target="tpu_custom_call" | custom-call | flops 335544320 | bytes 1048576 | tf_op jit(solution)/shard_map/boundary/pallas_call | solution.py:321

commit v7 on v6

--- a/solution.py
+++ b/solution.py
@@ -10,8 +10,6 @@
 
 ROWS = 8
 CHUNKS = 4
-FULL = 3
-GROUP = 4
 MESH = pl.DeviceIdType.MESH
 
 
@@ -59,11 +57,11 @@
     return result.reshape(len(rows), -1, result.shape[-1])
 
 
-def send_and_interior(
+def kronecker_product(
     count, scaling,
     signal_ref, tiles_ref, tree_ref, send_ref, column_ref,
-    product, xs, a, weights, quad_ref,
-    x, tiles, tree_in, send_in, column_in, extended, pull, outgoing, received, shares,
+    product, quad_ref,
+    x, tiles, tree_in, send_in, column_in, xs, a, extended, pull, outgoing, received, shares,
     x_sem, small_sem, tiles_sem, send_sem, recv_sem, share_send, share_recv,
 ):
     tile_rows, nodes, species = x.shape
@@ -74,9 +72,7 @@
     load_x = pltpu.make_async_copy(signal_ref, x, x_sem)
     load_x.start()
     load_tree = pltpu.make_async_copy(tree_ref, tree_in, small_sem.at[1])
-    load_tree.start()
     load_column = pltpu.make_async_copy(column_ref, column_in, small_sem.at[2])
-    load_column.start()
     wide = count // ROWS
     me = lax.axis_index("space")
     column, row = lax.rem(me, wide), me // wide
@@ -91,7 +87,6 @@
     for c in range(CHUNKS):
         piece = pl.ds(c * part, part)
         loads.append(pltpu.make_async_copy(tiles_ref.at[piece], tiles.at[piece], tiles_sem.at[c]))
-        loads[-1].start()
 
     barrier = pltpu.get_barrier_semaphore()
 
@@ -101,6 +96,10 @@
 
     load_send.wait()
     load_x.wait()
+    load_tree.start()
+    load_column.start()
+    for load in loads:
+        load.start()
 
     def copy_for(d):
         return pltpu.make_async_remote_copy(
@@ -126,7 +125,6 @@
     tree = tree_in[...]
     right, right_t = doubled(tree), doubled(tree.T)
 
-    weights[...] = right_t
     load_column.wait()
 
     for load in loads:
@@ -164,21 +162,6 @@
 
     lax.fori_loop(0, CHUNKS, prepare, 0)
 
-    def multiply(c, last):
-        first = c * part
-        piece = pl.ds(first, part)
-        named = [
-            [jnp.minimum(column_in[k, first + t], last) for k in range(stored)]
-            for t in range(part)
-        ]
-        product[piece] = rows_product(a.at[piece], named, xs, right_t)
-
-    def interior(c, carry):
-        multiply(c, tile_rows - 1)
-        return carry
-
-    lax.fori_loop(FULL, CHUNKS, interior, 0)
-
     for d in (0, 1, 2, 3):
         @pl.when(receives[d])
         def _():
@@ -212,11 +195,14 @@
     for copy in copies:
         copy.start()
 
-    def full(c, carry):
-        multiply(c, xs.shape[0] - 1)
+    def multiply(c, carry):
+        first = c * part
+        piece = pl.ds(first, part)
+        named = [[column_in[k, first + t] for k in range(stored)] for t in range(part)]
+        product[piece] = rows_product(a.at[piece], named, xs, right_t)
         return carry
 
-    lax.fori_loop(0, FULL, full, 0)
+    lax.fori_loop(0, CHUNKS, multiply, 0)
 
     for d in range(4):
         @pl.when(sends[d])
@@ -227,38 +213,6 @@
     quad_ref[0] = jnp.sum(jnp.sum(shares[...], axis=0)) * scaling
     for copy in copies:
         copy.wait_send()
-
-
-def boundary(
-    done, interior, xs, a, weights, columns_ref, product_ref, again, columns, column_sem, out_sem,
-):
-    tile_rows = interior.shape[0]
-    stored = columns.shape[0]
-    load = pltpu.make_async_copy(columns_ref, columns, column_sem)
-    load.start()
-    final = pl.ds(0, done)
-    pltpu.make_async_copy(interior.at[final], product_ref.at[final], out_sem).start()
-    load.wait()
-
-    def group(g, carry):
-        first = g * GROUP
-        piece = pl.ds(first, GROUP)
-        named = [[columns[k, first + t] for k in range(stored)] for t in range(GROUP)]
-        furthest = functools.reduce(jnp.maximum, [c for row in named for c in row])
-
-        @pl.when(furthest >= tile_rows)
-        def _():
-            again[piece] = rows_product(a.at[piece], named, xs, weights[...])
-            pltpu.make_async_copy(again.at[piece], product_ref.at[piece], out_sem).start()
-
-        @pl.when(furthest < tile_rows)
-        def _():
-            pltpu.make_async_copy(interior.at[piece], product_ref.at[piece], out_sem).start()
-
-        return carry
-
-    lax.fori_loop(done // GROUP, tile_rows // GROUP, group, 0)
-    pltpu.make_async_copy(again, product_ref, out_sem).wait()
 
 
 def on_device(signal, space_tiles, tree_precision, send_tiles, column_tiles):
@@ -277,23 +231,19 @@
     lists = (directions, capacity, nodes, species)
     columns = column_tiles.T
     flops = 2 * tile_rows * nodes * species * (width + 2 * species)
-    between = (
-        vmem(field, f32),
-        vmem((tile_rows + directions * capacity, nodes, 2 * species), bf16),
-        vmem((tile_rows, 2 * nodes, width), bf16),
-        vmem((2 * species, 2 * species), bf16),
-    )
-    *kept, quad = pl.pallas_call(
-        functools.partial(send_and_interior, count, scaling),
-        out_shape=(*between, jax.ShapeDtypeStruct((1,), f32)),
+    product, quad = pl.pallas_call(
+        functools.partial(kronecker_product, count, scaling),
+        out_shape=(vmem(field, f32), jax.ShapeDtypeStruct((1,), f32)),
         in_specs=[hbm] * 5,
-        out_specs=(near,) * len(between) + (smem,),
+        out_specs=(near, smem),
         scratch_shapes=[
             vmem(field, f32),
             vmem(space_tiles.shape, f32),
             vmem(tree_precision.shape, f32),
             pltpu.SMEM((directions, capacity), jnp.int32),
             pltpu.SMEM(columns.shape, jnp.int32),
+            vmem((tile_rows + directions * capacity, nodes, 2 * species), bf16),
+            vmem((tile_rows, 2 * nodes, width), bf16),
             vmem((tile_rows + directions * capacity, nodes, species), f32),
             vmem((tile_rows, stored, nodes, species), f32),
             vmem(lists, f32),
@@ -308,28 +258,16 @@
             dma((count,)),
         ],
         compiler_params=pltpu.CompilerParams(
-            collective_id=0, has_side_effects=True, vmem_limit_bytes=32 * 2**20
+            collective_id=0, has_side_effects=True, vmem_limit_bytes=40 * 2**20
         ),
         cost_estimate=pl.CostEstimate(
             flops=flops, bytes_accessed=4 * (space_tiles.size + signal.size), transcendentals=0
         ),
-        name="send_and_interior",
+        name="kronecker_product",
     )(*(
         pltpu.with_memory_space_constraint(array, pltpu.HBM)
         for array in (signal.reshape(field), space_tiles, tree_precision, send_tiles[0], columns)
     ))
-    product = pl.pallas_call(
-        functools.partial(boundary, tile_rows // CHUNKS * FULL),
-        out_shape=jax.ShapeDtypeStruct(field, f32),
-        in_specs=[near] * len(between) + [hbm],
-        out_specs=hbm,
-        scratch_shapes=[vmem(field, f32), pltpu.SMEM(columns.shape, jnp.int32), dma, dma],
-        compiler_params=pltpu.CompilerParams(vmem_limit_bytes=16 * 2**20),
-        cost_estimate=pl.CostEstimate(
-            flops=flops, bytes_accessed=4 * signal.size, transcendentals=0
-        ),
-        name="boundary",
-    )(*kept, pltpu.with_memory_space_constraint(columns, pltpu.HBM))
     return product.reshape(signal.shape), quad
 
 

time: 28.1 us -> 27.6 us (0.982)
  Pallas kernels: 25.6 us -> 24.2 us
  local copies, waits for them, and re-layouts: 0 us -> 0.97 us
    pallas_call x2 -> x1, Pallas kernels: 25.6 us -> 24.2 us  [on_device(): pl.pallas_call(functools.partial(kronecker_product, count, scaling), out_...]
    unnamed x0 -> x1, local copies, waits for them, and re-layouts: none -> 0.97 us
where the time goes in v7:
time: 27.6 us; the launch traced here: 27.5 us
  Pallas kernels  24.2 us (88%)
  between operations  2.33 us (8%)
  local copies, waits for them, and re-layouts  0.97 us (4%)
    pallas_call x1, Pallas kernels, on_device(): pl.pallas_call(functools.partial(kronecker_product, count, scaling), out_...  24.2 us
    unnamed x1, local copies, waits for them, and re-layouts  0.97 us

profile of v7, /device:TPU:0, one launch (start us, length us, event | category | flops | bytes accessed | tf_op | source)
XLA Modules:
  0.0 27.5 jit_solution(2285023588936718799)
XLA Ops:
  0.6 24.2 %kronecker_product.1 = (f32[32,64,128]{2,1,0:T(8,128)S(1)}, f32[1]{0:T(128)}) custom-call(f32[32,64,128]{2,1,0:T(8,128)} %bitcast.5, f32[32,64,384]{2,1,0:T(8,128)} %tiles_ref.1, f32[128,128]{1,0:T(8,128)} %tree_ref.1, s32[4,8]{1,0:T(4,128)} %bitcast.7, s32[6,32]{1,0:T(8,128)} %bitcast.6), custom_call_target="tpu_custom_call" | custom-call | flops 335544320 | bytes 4194304 | tf_op jit(solution)/shard_map/kronecker_product/pallas_call | solution.py:234
  24.8 1.0 %copy.9 = f32[2048,128]{1,0:T(8,128)} copy(f32[2048,128]{1,0:T(8,128)S(1)} %bitcast.4) | data formatting | bytes 2097152

commit v8 on v7

--- a/solution.py
+++ b/solution.py
@@ -10,6 +10,7 @@
 
 ROWS = 8
 CHUNKS = 4
+PIECES = 4
 MESH = pl.DeviceIdType.MESH
 
 
@@ -101,12 +102,15 @@
     for load in loads:
         load.start()
 
-    def copy_for(d):
+    size = capacity // PIECES
+
+    def copy_for(d, piece):
+        slots = pl.ds(piece * size, size)
         return pltpu.make_async_remote_copy(
-            src_ref=outgoing.at[d],
-            dst_ref=received.at[d],
-            send_sem=send_sem.at[d],
-            recv_sem=recv_sem.at[d],
+            src_ref=outgoing.at[d, slots],
+            dst_ref=received.at[d, slots],
+            send_sem=send_sem.at[d, piece],
+            recv_sem=recv_sem.at[d, piece],
             device_id={"space": targets[d]},
             device_id_type=MESH,
         )
@@ -114,12 +118,18 @@
     for d in (2, 3, 0, 1):
         for j in range(capacity):
             outgoing[d, j] = x[send_in[d, j]]
-        if d == 2:
+        if d == 3:
             pl.semaphore_wait(barrier, count - 1)
-
+            for piece in range(PIECES):
+                for e in (2, 3):
+                    @pl.when(sends[e])
+                    def _():
+                        copy_for(e, piece).start()
+    for d in (0, 1):
         @pl.when(sends[d])
         def _():
-            copy_for(d).start()
+            for piece in range(PIECES):
+                copy_for(d, piece).start()
 
     load_tree.wait()
     tree = tree_in[...]
@@ -162,25 +172,33 @@
 
     lax.fori_loop(0, CHUNKS, prepare, 0)
 
-    for d in (0, 1, 2, 3):
+    def own_entry(t, acc):
+        term = pull[t, 0] * x[t]
+        return acc + jnp.sum(term.reshape(nodes // 8, 8, species), axis=0)
+
+    acc = lax.fori_loop(
+        0, tile_rows, own_entry, jnp.zeros((8, species), jnp.float32), unroll=4
+    )
+
+    order = [(d, piece) for d in (0, 1) for piece in range(PIECES)]
+    order += [(d, piece) for piece in range(PIECES) for d in (2, 3)]
+    for d, piece in order:
         @pl.when(receives[d])
         def _():
-            copy_for(d).wait_recv()
-            for j in range(capacity):
+            copy_for(d, piece).wait_recv()
+            for j in range(piece * size, (piece + 1) * size):
                 tile = received[d, j]
                 extended[tile_rows + d * capacity + j] = tile
                 high, low = halves(tile)
                 xs[tile_rows + d * capacity + j] = jnp.concatenate([high, low], 1)
 
     def weigh(t, acc):
-        for k in range(stored):
+        for k in range(1, stored):
             term = pull[t, k] * extended[column_in[k, t]]
             acc = acc + jnp.sum(term.reshape(nodes // 8, 8, species), axis=0)
         return acc
 
-    shares[me] = lax.fori_loop(
-        0, tile_rows, weigh, jnp.zeros((8, species), jnp.float32), unroll=4
-    )
+    shares[me] = lax.fori_loop(0, tile_rows, weigh, acc, unroll=4)
     copies = [
         pltpu.make_async_remote_copy(
             src_ref=shares.at[me],
@@ -207,7 +225,8 @@
     for d in range(4):
         @pl.when(sends[d])
         def _():
-            copy_for(d).wait_send()
+            for piece in range(PIECES):
+                copy_for(d, piece).wait_send()
     for copy in copies:
         copy.wait_recv()
     quad_ref[0] = jnp.sum(jnp.sum(shares[...], axis=0)) * scaling
@@ -252,8 +271,8 @@
             dma,
             dma((3,)),
             dma((CHUNKS,)),
-            dma((directions,)),
-            dma((directions,)),
+            dma((directions, PIECES)),
+            dma((directions, PIECES)),
             dma((count,)),
             dma((count,)),
         ],

time: 27.6 us -> 27.7 us (level)
  no operation moved by 1% of the time
where the time goes in v8:
time: 27.7 us; the launch traced here: 27.6 us
  Pallas kernels  24.3 us (88%)
  between operations  2.33 us (8%)
  local copies, waits for them, and re-layouts  0.97 us (4%)
    pallas_call x1, Pallas kernels, on_device(): pl.pallas_call(functools.partial(kronecker_product, count, scaling), out_...  24.3 us
    unnamed x1, local copies, waits for them, and re-layouts  0.97 us

profile of v8, /device:TPU:0, one launch (start us, length us, event | category | flops | bytes accessed | tf_op | source)
XLA Modules:
  0.0 27.6 jit_solution(9711480828369858896)
XLA Ops:
  0.6 24.3 %kronecker_product.1 = (f32[32,64,128]{2,1,0:T(8,128)S(1)}, f32[1]{0:T(128)}) custom-call(f32[32,64,128]{2,1,0:T(8,128)} %bitcast.5, f32[32,64,384]{2,1,0:T(8,128)} %tiles_ref.1, f32[128,128]{1,0:T(8,128)} %tree_ref.1, s32[4,8]{1,0:T(4,128)} %bitcast.7, s32[6,32]{1,0:T(8,128)} %bitcast.6), custom_call_target="tpu_custom_call" | custom-call | flops 335544320 | bytes 4194304 | tf_op jit(solution)/shard_map/kronecker_product/pallas_call | solution.py:253
  24.9 1.0 %copy.9 = f32[2048,128]{1,0:T(8,128)} copy(f32[2048,128]{1,0:T(8,128)S(1)} %bitcast.4) | data formatting | bytes 2097152

commit v9 on v8

--- a/solution.py
+++ b/solution.py
@@ -62,8 +62,8 @@
     count, scaling,
     signal_ref, tiles_ref, tree_ref, send_ref, column_ref,
     product, quad_ref,
-    x, tiles, tree_in, send_in, column_in, xs, a, extended, pull, outgoing, received, shares,
-    x_sem, small_sem, tiles_sem, send_sem, recv_sem, share_send, share_recv,
+    x, tiles, tree_in, send_in, column_in, xs, a, extended, pull, outgoing, received, inner_shares, outer_shares,
+    x_sem, small_sem, tiles_sem, send_sem, recv_sem, inner_send, inner_recv, outer_send, outer_recv,
 ):
     tile_rows, nodes, species = x.shape
     stored = column_ref.shape[0]
@@ -91,9 +91,18 @@
 
     barrier = pltpu.get_barrier_semaphore()
 
-    others = [lax.rem(me + i, count) for i in range(1, count)]
-    for device in others:
+    def greet(device):
         pl.semaphore_signal(barrier, inc=1, device_id={"space": device}, device_id_type=MESH)
+
+    for d in (2, 3, 0, 1):
+        pl.when(sends[d])(functools.partial(greet, targets[d]))
+    inner, outer = inner_shares.shape[0], outer_shares.shape[0]
+    spot, team = lax.rem(me, inner), me // inner
+    mates = [team * inner + lax.rem(spot + i, inner) for i in range(1, inner)]
+    peers = [spot + inner * lax.rem(team + i, outer) for i in range(1, outer)]
+    for device in peers + mates:
+        greet(device)
+    greeted = len(mates) + len(peers) + sum(jnp.where(has, 1, 0) for has in receives)
 
     load_send.wait()
     load_x.wait()
@@ -119,7 +128,7 @@
         for j in range(capacity):
             outgoing[d, j] = x[send_in[d, j]]
         if d == 3:
-            pl.semaphore_wait(barrier, count - 1)
+            pl.semaphore_wait(barrier, greeted)
             for piece in range(PIECES):
                 for e in (2, 3):
                     @pl.when(sends[e])
@@ -198,39 +207,49 @@
             acc = acc + jnp.sum(term.reshape(nodes // 8, 8, species), axis=0)
         return acc
 
-    shares[me] = lax.fori_loop(0, tile_rows, weigh, acc, unroll=4)
-    copies = [
-        pltpu.make_async_remote_copy(
-            src_ref=shares.at[me],
-            dst_ref=shares.at[me],
-            send_sem=share_send.at[i],
-            recv_sem=share_recv.at[i],
-            device_id={"space": device},
-            device_id_type=MESH,
-        )
-        for i, device in enumerate(others)
-    ]
-    for copy in copies:
+    inner_shares[spot] = lax.fori_loop(0, tile_rows, weigh, acc, unroll=4)
+    def share_copies(shares, mine, send, receive, devices):
+        return [
+            pltpu.make_async_remote_copy(
+                src_ref=shares.at[mine],
+                dst_ref=shares.at[mine],
+                send_sem=send.at[i],
+                recv_sem=receive.at[i],
+                device_id={"space": device},
+                device_id_type=MESH,
+            )
+            for i, device in enumerate(devices)
+        ]
+
+    first = share_copies(inner_shares, spot, inner_send, inner_recv, mates)
+    second = share_copies(outer_shares, team, outer_send, outer_recv, peers)
+    for copy in first:
         copy.start()
 
     def multiply(c, carry):
-        first = c * part
-        piece = pl.ds(first, part)
-        named = [[column_in[k, first + t] for k in range(stored)] for t in range(part)]
+        start = c * part
+        piece = pl.ds(start, part)
+        named = [[column_in[k, start + t] for k in range(stored)] for t in range(part)]
         product[piece] = rows_product(a.at[piece], named, xs, right_t)
         return carry
 
-    lax.fori_loop(0, CHUNKS, multiply, 0)
+    lax.fori_loop(0, 1, multiply, 0)
+    for copy in first:
+        copy.wait_recv()
+    outer_shares[team] = jnp.sum(inner_shares[...], axis=0)
+    for copy in second:
+        copy.start()
+    lax.fori_loop(1, CHUNKS, multiply, 0)
 
     for d in range(4):
         @pl.when(sends[d])
         def _():
             for piece in range(PIECES):
                 copy_for(d, piece).wait_send()
-    for copy in copies:
+    for copy in second:
         copy.wait_recv()
-    quad_ref[0] = jnp.sum(jnp.sum(shares[...], axis=0)) * scaling
-    for copy in copies:
+    quad_ref[0] = jnp.sum(jnp.sum(outer_shares[...], axis=0)) * scaling
+    for copy in first + second:
         copy.wait_send()
 
 
@@ -240,6 +259,7 @@
     stored = column_tiles.shape[1]
     species = signal.shape[1]
     directions, capacity = send_tiles.shape[1:]
+    inner = max(i for i in range(1, math.isqrt(count) + 1) if count % i == 0)
     scaling = 1.0 / math.sqrt(count * tile_rows * nodes * species)
     vmem, f32, bf16 = pltpu.VMEM, jnp.float32, jnp.bfloat16
     dma = pltpu.SemaphoreType.DMA
@@ -267,14 +287,17 @@
             vmem((tile_rows, stored, nodes, species), f32),
             vmem(lists, f32),
             vmem(lists, f32),
-            vmem((count, 8, species), f32),
+            vmem((inner, 8, species), f32),
+            vmem((count // inner, 8, species), f32),
             dma,
             dma((3,)),
             dma((CHUNKS,)),
             dma((directions, PIECES)),
             dma((directions, PIECES)),
-            dma((count,)),
-            dma((count,)),
+            dma((inner,)),
+            dma((inner,)),
+            dma((count // inner,)),
+            dma((count // inner,)),
         ],
         compiler_params=pltpu.CompilerParams(
             collective_id=0, has_side_effects=True, vmem_limit_bytes=40 * 2**20

time: 27.7 us -> 28.3 us (1.022)
  Pallas kernels: 24.3 us -> 24.8 us
    pallas_call x1, Pallas kernels: 24.3 us -> 24.8 us  [on_device(): pl.pallas_call(functools.partial(kronecker_product, count, scaling), out_...]
where the time goes in v9:
time: 28.3 us; the launch traced here: 28.1 us
  Pallas kernels  24.8 us (88%)
  between operations  2.33 us (8%)
  local copies, waits for them, and re-layouts  0.97 us (3%)
    pallas_call x1, Pallas kernels, on_device(): pl.pallas_call(functools.partial(kronecker_product, count, scaling), out_...  24.8 us
    unnamed x1, local copies, waits for them, and re-layouts  0.97 us

profile of v9, /device:TPU:0, one launch (start us, length us, event | category | flops | bytes accessed | tf_op | source)
XLA Modules:
  0.0 28.1 jit_solution(11119495903238134245)
XLA Ops:
  0.6 24.8 %kronecker_product.1 = (f32[32,64,128]{2,1,0:T(8,128)S(1)}, f32[1]{0:T(128)}) custom-call(f32[32,64,128]{2,1,0:T(8,128)} %bitcast.5, f32[32,64,384]{2,1,0:T(8,128)} %tiles_ref.1, f32[128,128]{1,0:T(8,128)} %tree_ref.1, s32[4,8]{1,0:T(4,128)} %bitcast.7, s32[6,32]{1,0:T(8,128)} %bitcast.6), custom_call_target="tpu_custom_call" | custom-call | flops 335544320 | bytes 4194304 | tf_op jit(solution)/shard_map/kronecker_product/pallas_call | solution.py:273
  25.5 1.0 %copy.9 = f32[2048,128]{1,0:T(8,128)} copy(f32[2048,128]{1,0:T(8,128)S(1)} %bitcast.4) | data formatting | bytes 2097152

commit v10 on v8

--- a/solution.py
+++ b/solution.py
@@ -91,7 +91,9 @@
 
     barrier = pltpu.get_barrier_semaphore()
 
-    others = [lax.rem(me + i, count) for i in range(1, count)]
+    near = [wide, count - wide, 1, count - 1]
+    far = [i for i in range(1, count) if i not in near]
+    others = [lax.rem(me + i, count) for i in dict.fromkeys(near + far)]
     for device in others:
         pl.semaphore_signal(barrier, inc=1, device_id={"space": device}, device_id_type=MESH)
 
@@ -229,7 +231,8 @@
                 copy_for(d, piece).wait_send()
     for copy in copies:
         copy.wait_recv()
-    quad_ref[0] = jnp.sum(jnp.sum(shares[...], axis=0)) * scaling
+    total = jnp.sum(shares[...], axis=0)
+    quad_ref[...] = jnp.sum(total, axis=(0, 1), keepdims=True) * scaling
     for copy in copies:
         copy.wait_send()
 
@@ -245,16 +248,15 @@
     dma = pltpu.SemaphoreType.DMA
     hbm = pl.BlockSpec(memory_space=pltpu.HBM)
     near = pl.BlockSpec(memory_space=vmem)
-    smem = pl.BlockSpec(memory_space=pltpu.SMEM)
     field = (tile_rows, nodes, species)
     lists = (directions, capacity, nodes, species)
     columns = column_tiles.T
     flops = 2 * tile_rows * nodes * species * (width + 2 * species)
     product, quad = pl.pallas_call(
         functools.partial(kronecker_product, count, scaling),
-        out_shape=(vmem(field, f32), jax.ShapeDtypeStruct((1,), f32)),
+        out_shape=(vmem(field, f32), vmem((1, 1), f32)),
         in_specs=[hbm] * 5,
-        out_specs=(near, smem),
+        out_specs=(near, near),
         scratch_shapes=[
             vmem(field, f32),
             vmem(space_tiles.shape, f32),
@@ -287,7 +289,7 @@
         pltpu.with_memory_space_constraint(array, pltpu.HBM)
         for array in (signal.reshape(field), space_tiles, tree_precision, send_tiles[0], columns)
     ))
-    return product.reshape(signal.shape), quad
+    return product.reshape(signal.shape), quad.reshape(1)
 
 
 def solution(mesh):

time: 27.7 us -> 26.6 us (0.960)
  Pallas kernels: 24.3 us -> 23.7 us
  between operations: 2.33 us -> 1.8 us
    pallas_call x1, Pallas kernels: 24.3 us -> 23.7 us  [on_device(): pl.pallas_call(functools.partial(kronecker_product, count, scaling), out_...]
where the time goes in v10:
time: 26.6 us; the launch traced here: 26.5 us
  Pallas kernels  23.7 us (89%)
  between operations  1.8 us (7%)
  local copies, waits for them, and re-layouts  0.97 us (4%)
    pallas_call x1, Pallas kernels, on_device(): pl.pallas_call(functools.partial(kronecker_product, count, scaling), out_...  23.7 us
    unnamed x1, local copies, waits for them, and re-layouts  0.97 us

profile of v10, /device:TPU:0, one launch (start us, length us, event | category | flops | bytes accessed | tf_op | source)
XLA Modules:
  0.0 26.5 jit_solution(16335431150247573387)
XLA Ops:
  0.6 23.7 %kronecker_product.1 = (f32[32,64,128]{2,1,0:T(8,128)S(1)}, f32[1,1]{1,0:T(1,128)S(1)}) custom-call(f32[32,64,128]{2,1,0:T(8,128)} %bitcast.6, f32[32,64,384]{2,1,0:T(8,128)} %tiles_ref.1, f32[128,128]{1,0:T(8,128)} %tree_ref.1, s32[4,8]{1,0:T(4,128)} %bitcast.8, s32[6,32]{1,0:T(8,128)} %bitcast.7), custom_call_target="tpu_custom_call" | custom-call | flops 335544320 | bytes 4194304 | tf_op jit(solution)/shard_map/kronecker_product/pallas_call | solution.py:255
  24.4 1.0 %copy.9 = f32[2048,128]{1,0:T(8,128)} copy(f32[2048,128]{1,0:T(8,128)S(1)} %bitcast.5) | data formatting | bytes 2097152

commit v11 on v10

--- a/solution.py
+++ b/solution.py
@@ -212,7 +212,7 @@
         )
         for i, device in enumerate(others)
     ]
-    for copy in copies:
+    for copy in reversed(copies):
         copy.start()
 
     def multiply(c, carry):

time: 26.6 us -> 26.8 us (level)
  no operation moved by 1% of the time
where the time goes in v11:
time: 26.8 us; the launch traced here: 26.6 us
  Pallas kernels  23.8 us (89%)
  between operations  1.8 us (7%)
  local copies, waits for them, and re-layouts  0.97 us (4%)
    pallas_call x1, Pallas kernels, on_device(): pl.pallas_call(functools.partial(kronecker_product, count, scaling), out_...  23.8 us
    unnamed x1, local copies, waits for them, and re-layouts  0.97 us

profile of v11, /device:TPU:0, one launch (start us, length us, event | category | flops | bytes accessed | tf_op | source)
XLA Modules:
  0.0 26.6 jit_solution(10133493980141915495)
XLA Ops:
  0.6 23.8 %kronecker_product.1 = (f32[32,64,128]{2,1,0:T(8,128)S(1)}, f32[1,1]{1,0:T(1,128)S(1)}) custom-call(f32[32,64,128]{2,1,0:T(8,128)} %bitcast.6, f32[32,64,384]{2,1,0:T(8,128)} %tiles_ref.1, f32[128,128]{1,0:T(8,128)} %tree_ref.1, s32[4,8]{1,0:T(4,128)} %bitcast.8, s32[6,32]{1,0:T(8,128)} %bitcast.7), custom_call_target="tpu_custom_call" | custom-call | flops 335544320 | bytes 4194304 | tf_op jit(solution)/shard_map/kronecker_product/pallas_call | solution.py:255
  24.5 1.0 %copy.9 = f32[2048,128]{1,0:T(8,128)} copy(f32[2048,128]{1,0:T(8,128)S(1)} %bitcast.5) | data formatting | bytes 2097152
